TPU v7x, 512 devices: a whole 4x4x16 slice. The times are simulated.
512 devices in a mesh: store: 32 (over z, core), feat: 16 (over y, x).
Axes of the slice: x: 4, y: 4, z: 16, core: 2. Of those that a mesh axis runs over, the one named last changes fastest.
Arguments:
- features: float32 [768, 131072], P('feat', 'store'), may hold values from -6 to 6
- serve_rows: int32 [32, 32, 256], P('store'), may hold values from 0 to 4095
- row_counts: int32 [32, 32], P('store'), may hold values from 1 to 256, as said below
- layer1_index: int32 [32, 11, 512], P('store'), may hold values from 0 to 8191
- layer2_index: int32 [32, 16, 512], P('store'), may hold values from 0 to 511
- w1_self: bfloat16 [768, 1024], P('feat'), may hold values from -0.21875 to 0.21875
- w1_neigh: bfloat16 [768, 1024], P('feat'), may hold values from -0.21875 to 0.21875
- w2_self_t: bfloat16 [1024, 1024], P('feat'), may hold values from -0.1875 to 0.1875
- w2_neigh_t: bfloat16 [1024, 1024], P('feat'), may hold values from -0.1875 to 0.1875
- out_grad: bfloat16 [1024, 16384], P('feat', 'store'), may hold values from -0.1875 to 0.1875
Outputs:
- h2: bfloat16 [1024, 16384], P('feat', 'store')
- grad_w1_self: float32 [768, 1024], P('feat')
- grad_w1_neigh: float32 [768, 1024], P('feat')
- grad_w2_self_t: float32 [1024, 1024], P('feat')
- grad_w2_neigh_t: float32 [1024, 1024], P('feat')
Inputs may be any that keep to these rules, and one draw needn't show every extreme that they name: Of the 256 slots that owner o fills for trainer t, the first row_counts[t, o] are used; in every draw some trainer uses all 256 slots of every owner.
All inputs are finite; a program needn't handle non-finite values.
Results may differ from a plain program's by a relative error of at most 0.009.
Values may be sent and summed in bfloat16 or wider, within the bound.
A program may use at most 64 MiB of HBM per device.

v0:
```python
import jax
import jax.numpy as jnp
from jax import lax
from jax.sharding import PartitionSpec as P


def silu_slope(values):
    sigma_val = jax.nn.sigmoid(values)
    return sigma_val * (1.0 + values * (1.0 - sigma_val))


def contract_rows(left, right):
    return lax.dot_general(
        left, right, (((0,), (0,)), ((), ())), preferred_element_type=jnp.float32
    )


def contract_last(left, right):
    return lax.dot_general(
        left, right, (((1,), (1,)), ((), ())), preferred_element_type=jnp.float32
    )


def split_product(values, weights):
    upper = values.astype(jnp.bfloat16)
    lower = (values - upper.astype(jnp.float32)).astype(jnp.bfloat16)
    return jnp.dot(upper, weights, preferred_element_type=jnp.float32) + jnp.dot(
        lower, weights, preferred_element_type=jnp.float32
    )


def body(
    features,
    serve_rows,
    row_counts,
    layer1_index,
    layer2_index,
    w1_self,
    w1_neigh,
    w2_self_t,
    w2_neigh_t,
    out_grad,
):
    slot_cap = serve_rows.shape[2]
    chosen = jnp.take(features, serve_rows[0].reshape(-1), axis=1)
    inputs = lax.all_to_all(chosen, "store", split_axis=1, concat_axis=1, tiled=True)
    raw_index = layer1_index[0]
    owner_ids = raw_index // slot_cap
    slot_ids = owner_ids * slot_cap + raw_index % slot_cap % jnp.take(row_counts[0], owner_ids)
    fetched = jnp.take(inputs, slot_ids, axis=1)
    fan_one = raw_index.shape[0] - 1
    self_one = fetched[:, 0].astype(jnp.bfloat16)
    neigh_one = (jnp.sum(fetched[:, 1:], axis=1) / fan_one).astype(jnp.bfloat16)
    node_count = raw_index.shape[1]
    self_rows, neigh_rows = (
        lax.all_to_all(self_one, "feat", split_axis=1, concat_axis=0, tiled=True),
        lax.all_to_all(neigh_one, "feat", split_axis=1, concat_axis=0, tiled=True),
    )
    self_part = self_rows
    neigh_part = neigh_rows
    pre_one = contract_rows(
        self_part, lax.all_gather(w1_self, "feat", axis=0, tiled=True)
    ) + contract_rows(neigh_part, lax.all_gather(w1_neigh, "feat", axis=0, tiled=True))
    hid_block = jax.nn.silu(pre_one).astype(jnp.bfloat16)
    hid_one = lax.all_gather(hid_block, "feat", axis=0, tiled=True)
    index_two = layer2_index[0]
    fan_two = index_two.shape[0] - 1
    node_ids = lax.broadcasted_iota(jnp.int32, (1, 1, node_count), 2)
    count_table = jnp.sum((index_two[1:, :, None] == node_ids).astype(jnp.float32), axis=0).astype(
        jnp.bfloat16
    )
    self_table = (index_two[0][:, None] == node_ids[0]).astype(jnp.bfloat16)
    self_two = jnp.take(hid_one, index_two[0], axis=0)
    neigh_two = (
        jnp.dot(count_table, hid_one, preferred_element_type=jnp.float32) / fan_two
    ).astype(jnp.bfloat16)
    pre_two = contract_last(w2_self_t, self_two) + contract_last(w2_neigh_t, neigh_two)
    out_block = jax.nn.silu(pre_two).astype(jnp.bfloat16)
    grad_pre_two = (out_grad.astype(jnp.float32) * silu_slope(pre_two)).astype(jnp.bfloat16)
    grad_w2s = jnp.dot(grad_pre_two, self_two, preferred_element_type=jnp.float32)
    grad_w2n = jnp.dot(grad_pre_two, neigh_two, preferred_element_type=jnp.float32)
    node_self = contract_last(self_table.T, grad_pre_two)
    node_neigh = contract_last(count_table.T, grad_pre_two) / fan_two
    back_full = split_product(node_self, w2_self_t) + split_product(node_neigh, w2_neigh_t)
    grad_block = lax.psum_scatter(back_full, "feat", scatter_dimension=0, tiled=True)
    grad_pre_one = (grad_block * silu_slope(pre_one)).astype(jnp.bfloat16)
    piece = lax.all_gather(grad_pre_one, "feat", axis=0, tiled=True)
    self_part = self_one
    neigh_part = neigh_one
    grad_w1s = jnp.dot(self_part, piece, preferred_element_type=jnp.float32)
    grad_w1n = jnp.dot(neigh_part, piece, preferred_element_type=jnp.float32)
    reduced = lax.psum((grad_w1s, grad_w1n, grad_w2s, grad_w2n), "store")
    return (out_block, reduced[0], reduced[1], reduced[2], reduced[3])


def solution(mesh):
    return jax.shard_map(
        body,
        mesh=mesh,
        in_specs=(
            P("feat", "store"),
            P("store", None, None),
            P("store", None),
            P("store", None, None),
            P("store", None, None),
            P("feat", None),
            P("feat", None),
            P("feat", None),
            P("feat", None),
            P("feat", "store"),
        ),
        out_specs=(
            P("feat", "store"),
            P("feat", None),
            P("feat", None),
            P("feat", None),
            P("feat", None),
        ),
        check_vma=False,
    )
```

profile of v0, /device:TPU:1, one launch (start us, length us, event | category | flops | bytes accessed | tf_op | source)
XLA Modules:
  0.0 631.5 jit_solution(10167367748068472048)
XLA Ops:
  7.2 1.8 copy.30
  9.1 27.7 %gather_fusion.1 = f32[8192,48]{1,0:T(8,128)} fusion(f32[48,4096]{0,1:T(8,128)S(1)} %copy.30, s32[8192]{0:T(1024)S(1)} %broadcast_clamp_fusion), kind=kCustom, calls=%fused_computation.1 | custom fusion | bytes 3178496 | tf_op jit(solution)/shard_map/jit(_take)/gather | solution.py:45
  36.8 2.8 copy.31
  41.0 16.9 %all-to-all-start = ((f32[48,32,256]{2,0,1:T(8,128)}), f32[48,32,256]{2,0,1:T(8,128)S(1)}, u32[]{:S(2)}, u32[]{:S(2)}) async-start(f32[48,32,256]{2,0,1:T(8,128)} %broadcast_select_fusion.1), calls=%async_computation | async-start | bytes 3145728 | tf_op jit(solution)/shard_map/all_to_all | solution.py:46
  59.6 31.7 %gather_fusion = s32[5632]{0:T(1024)S(1)} fusion(s32[32]{0:T(128)S(1)} %bitcast.99, s32[6144]{0:T(1024)S(1)} %pad_clamp_fusion.1), kind=kCustom, calls=%fused_computation | custom fusion | bytes 67584 | tf_op jit(solution)/shard_map/jit(_take)/gather | solution.py:49
  91.3 2.0 fusion.21
  93.7 42.0 %all-to-all-done = f32[48,32,256]{2,0,1:T(8,128)S(1)} async-done(((f32[48,32,256]{2,0,1:T(8,128)}), f32[48,32,256]{2,0,1:T(8,128)S(1)}, u32[]{:S(2)}, u32[]{:S(2)}) %all-to-all-start) | async-done | bytes 1572896 | tf_op jit(solution)/shard_map/all_to_all | solution.py:46
  135.7 2.7 copy.32
  138.4 11.0 %gather_fusion.2 = f32[5632,48]{1,0:T(8,128)S(1)} fusion(f32[48,8192]{0,1:T(8,128)} %bitcast.100, s32[6144]{0:T(1024)S(1)} %pad_clamp_fusion), kind=kCustom, calls=%fused_computation.2 | custom fusion | bytes 2185216 | tf_op jit(solution)/shard_map/jit(_take)/gather | solution.py:50
  149.4 1.9 copy.33
  153.7 6.8 %all-to-all-start.2 = ((bf16[16,2,768]{2,1,0:T(2,128)(2,1)}), bf16[16,2,768]{2,1,0:T(2,128)(2,1)S(1)}, u32[]{:S(2)}, u32[]{:S(2)}) async-start(bf16[16,2,768]{2,1,0:T(2,128)(2,1)} %reshape.339), calls=%async_computation.2 | async-start | bytes 98304 | tf_op jit(solution)/shard_map/all_to_all | solution.py:57
  161.4 5.5 all-to-all-done.2
  166.9 3.5 all-to-all-start.1
  170.9 6.2 all-to-all-done.1
  177.6 1.8 fusion.27
  179.4 3.1 all-gather.7.cloned.1.call-done
  182.5 2.4 multiply_convert_fusion.4
  185.3 2.2 convert_reduce_fusion
  187.5 55.6 %all-gather.9.cloned.1.call-done = bf16[512,1024]{1,0:T(8,128)(2,1)} async-done(((bf16[32,1024]{1,0:T(8,128)(2,1)}), bf16[512,1024]{1,0:T(8,128)(2,1)}) %all-gather.9.cloned.1.call-update) | async-done | bytes 1048592 | tf_op jit(solution)/shard_map/all_gather | solution.py:65
  243.2 4.9 gather_fusion.3
  248.1 1.8 fusion.4
  253.7 1.8 add_add_fusion
  255.6 88.9 %reduce-scatter.2.cloned.1.call-done = f32[32,1024]{1,0:T(8,128)} async-done(((f32[512,1024]{1,0:T(8,128)}), f32[32,1024]{1,0:T(8,128)}) %reduce-scatter.2.cloned.1.call-update) | async-done | bytes 131088 | tf_op jit(solution)/shard_map/reduce_scatter | solution.py:85
  347.1 1.7 fusion.3
  348.8 57.1 %all-gather.11.cloned.1.call-done = bf16[512,1024]{1,0:T(8,128)(2,1)} async-done(((bf16[32,1024]{1,0:T(8,128)(2,1)}), bf16[512,1024]{1,0:T(8,128)(2,1)}) %all-gather.11.cloned.1.call-update) | async-done | bytes 1048592 | tf_op jit(solution)/shard_map/all_gather | solution.py:87
  406.0 2.2 fusion.28
  408.1 2.2 fusion.8
  410.4 207.7 %all-reduce.3.cloned.1.call-done = (f32[48,1024]{1,0:T(8,128)}, f32[48,1024]{1,0:T(8,128)}, f32[64,1024]{1,0:T(8,128)}, f32[64,1024]{1,0:T(8,128)}) async-done(((f32[48,1024]{1,0:T(8,128)}, f32[48,1024]{1,0:T(8,128)}, f32[64,1024]{1,0:T(8,128)}, f32[64,1024]{1,0:T(8,128)}), (f32[48,1024]{1,0:T(8,128)}, f32[48,1024]{1,0:T(8,128)}, f32[64,1024]{1,0:T(8,128)}, ...) | async-done | bytes 917520 | tf_op jit(solution)/shard_map/psum | solution.py:92
  618.1 1.6 copy.63
  619.7 1.6 copy.64
  621.3 1.7 copy.65
  623.0 1.7 copy.66
  (80 shorter events, 14.6 us)
Async XLA Ops:
  7.2 243.4 %copy-start = (bf16[64,1024]{1,0:T(8,128)(2,1)S(1)}, bf16[64,1024]{1,0:T(8,128)(2,1)}, u32[]{:S(2)}) copy-start(bf16[64,1024]{1,0:T(8,128)(2,1)} %param.18) | copy-start | bytes 393220
  7.2 1.8 copy-start.8
  41.0 18.4 %copy-start.7 = (s32[1,11,512]{2,0,1:T(1,128)S(1)}, s32[1,11,512]{2,0,1:T(1,128)}, u32[]{:S(2)}) copy-start(s32[1,11,512]{2,0,1:T(1,128)} %param.13) | copy-start | bytes 67588
  41.0 18.6 %copy-start.1 = (s32[1,32]{1,0:T(1,128)S(1)}, s32[1,32]{1,0:T(1,128)}, u32[]{:S(2)}) copy-start(s32[1,32]{1,0:T(1,128)} %param.12) | copy-start | bytes 388
  41.0 94.7 %all-to-all-start = ((f32[48,32,256]{2,0,1:T(8,128)}), f32[48,32,256]{2,0,1:T(8,128)S(1)}, u32[]{:S(2)}, u32[]{:S(2)}) async-start(f32[48,32,256]{2,0,1:T(8,128)} %broadcast_select_fusion.1), calls=%async_computation | async-start | bytes 3145728 | tf_op jit(solution)/shard_map/all_to_all | solution.py:46
  57.9 119.7 %all-gather.5.cloned.1.call-start = ((), (), s32[]{:S(2)}) async-start(), calls=%async_computation.4 | async-start | bytes 1671168 | tf_op jit(solution)/shard_map/all_gather | solution.py:62
  58.6 123.9 %all-gather.7.cloned.1.call-start = ((), (), s32[]{:S(2)}) async-start(), calls=%async_computation.5 | async-start | bytes 1671168 | tf_op jit(solution)/shard_map/all_gather | solution.py:63
  153.7 13.2 %all-to-all-start.2 = ((bf16[16,2,768]{2,1,0:T(2,128)(2,1)}), bf16[16,2,768]{2,1,0:T(2,128)(2,1)S(1)}, u32[]{:S(2)}, u32[]{:S(2)}) async-start(bf16[16,2,768]{2,1,0:T(2,128)(2,1)} %reshape.339), calls=%async_computation.2 | async-start | bytes 98304 | tf_op jit(solution)/shard_map/all_to_all | solution.py:57
  166.9 10.2 %all-to-all-start.1 = ((bf16[16,2,768]{2,1,0:T(2,128)(2,1)}), bf16[16,2,768]{2,1,0:T(2,128)(2,1)S(1)}, u32[]{:S(2)}, u32[]{:S(2)}) async-start(bf16[16,2,768]{2,1,0:T(2,128)(2,1)} %reshape.337), calls=%async_computation.1 | async-start | bytes 98304 | tf_op jit(solution)/shard_map/all_to_all | solution.py:56
  170.4 72.7 %all-gather.9.cloned.1.call-start = ((), (), s32[]{:S(2)}) async-start(), calls=%async_computation.6 | async-start | bytes 1114112 | tf_op jit(solution)/shard_map/all_gather | solution.py:65
  177.3 7.9 %copy-start.9 = (s32[1,16,512]{2,1,0:T(8,128)S(1)}, s32[1,16,512]{2,1,0:T(8,128)}, u32[]{:S(2)}) copy-start(s32[1,16,512]{2,1,0:T(8,128)} %param.14) | copy-start | bytes 98308
  185.0 159.4 %reduce-scatter.2.cloned.1.call-start = ((), (), s32[]{:S(2)}) async-start(), calls=%async_computation.7 | async-start | bytes 2228224 | tf_op jit(solution)/shard_map/reduce_scatter | solution.py:85
  185.3 62.8 %copy-start.10 = (pred[512]{0:T(512)(128)(4,1)}, pred[512]{0:T(512)(128)(4,1)S(1)}, u32[]{:S(2)}) copy-start(pred[512]{0:T(512)(128)(4,1)S(1)} %compare_and_fusion.2) | copy-start | bytes 1540
  187.5 60.5 %copy-start.6 = (bf16[64,1024]{1,0:T(8,128)(2,1)S(1)}, bf16[64,1024]{1,0:T(8,128)(2,1)}, u32[]{:S(2)}) copy-start(bf16[64,1024]{1,0:T(8,128)(2,1)} %param.17) | copy-start | bytes 393220
  243.1 6.7 %copy-start.2 = (bf16[512,1024]{1,0:T(8,128)(2,1)S(1)}, bf16[512,1024]{1,0:T(8,128)(2,1)}, u32[]{:S(2)}) copy-start(bf16[512,1024]{1,0:T(8,128)(2,1)} %all-gather.9.cloned.1.call-done) | copy-start | bytes 3145732
  248.1 2.5 copy-start.11
  250.6 2.0 copy-start.4
  255.5 90.6 %copy-start.5 = (bf16[512,1024]{1,0:T(8,128)(2,1)S(1)}, bf16[512,1024]{1,0:T(8,128)(2,1)}, u32[]{:S(2)}) copy-start(bf16[512,1024]{1,0:T(8,128)(2,1)} %copy-done.4) | copy-start | bytes 3145732
  255.5 91.6 %copy-start.3 = (bf16[512,1024]{1,0:T(8,128)(2,1)S(1)}, bf16[512,1024]{1,0:T(8,128)(2,1)}, u32[]{:S(2)}) copy-start(bf16[512,1024]{1,0:T(8,128)(2,1)} %gather_fusion.3) | copy-start | bytes 3145732
  255.5 150.4 %all-gather.11.cloned.1.call-start = ((), (), s32[]{:S(2)}) async-start(), calls=%async_computation.8 | async-start | bytes 1114112 | tf_op jit(solution)/shard_map/all_gather | solution.py:87
  346.0 272.0 %all-reduce.3.cloned.1.call-start = ((), (), s32[]{:S(2)}) async-start(), calls=%async_computation.9 | async-start | bytes 1835008 | tf_op jit(solution)/shard_map/psum | solution.py:92
Sparse Core Ops, SparseCore 0:
  61.7 59.0 all-gather.4
  123.8 58.6 all-gather.6
  186.1 56.9 all-gather.8
  255.6 88.7 reduce-scatter.1
  348.3 57.6 all-gather.10
  410.5 207.5 all-reduce.2
where the time goes:
time: 632 us
  waiting for transfers between devices  468 us (74%)
  local copies, waits for them, and re-layouts  93.8 us (15%)
  starting transfers between devices  27.6 us (4%)
  matrix products  18.7 us (3%)
  between operations  14.6 us (2%)
  other arithmetic  9.29 us (1%)
    psum x1, waiting for transfers between devices, body(): reduced = lax.psum((grad_w1s, grad_w1n, grad_w2s, grad_w2n), 'store')  208 us
    reduce_scatter x1, waiting for transfers between devices, body(): lax.psum_scatter(back_full, 'feat', scatter_dimension=0, tiled=True)  88.9 us
    all_gather x1, waiting for transfers between devices, body(): piece = lax.all_gather(grad_pre_one, 'feat', axis=0, tiled=True)  57.1 us
    all_gather x1, waiting for transfers between devices, body(): hid_one = lax.all_gather(hid_block, 'feat', axis=0, tiled=True)  55.6 us
    all_to_all x1, waiting for transfers between devices, body(): lax.all_to_all(chosen, 'store', split_axis=1, concat_axis=1, tiled=True)  42 us
    gather x3, local copies, waits for them, and re-layouts, body(): jnp.take(row_counts[0], owner_ids)  31.7 us
    gather x2, local copies, waits for them, and re-layouts, body(): chosen = jnp.take(features, serve_rows[0].reshape(-1), axis=1)  30.5 us
    all_to_all x1, starting transfers between devices, body(): lax.all_to_all(chosen, 'store', split_axis=1, concat_axis=1, tiled=True)  16.9 us
  transfers between devices with their start and end apart: 9, of which 8 were waited for; matrix products, arithmetic and copies ran while one was open for 10% of the time, Pallas kernels for 0%

commit v1 on v0

v1 whole, which is shorter than its diff:
```python
import functools

import jax
import jax.numpy as jnp
from jax import lax
from jax.experimental import pallas as pl
from jax.experimental.pallas import tpu as pltpu
from jax.sharding import PartitionSpec as P

MESH = pl.DeviceIdType.MESH
F32 = jnp.float32
BF16 = jnp.bfloat16
LOW = 256


def slope(values):
    sig = jax.nn.sigmoid(values)
    return sig * (1.0 + values * (1.0 - sig))


def nt_dot(left, right):
    return lax.dot_general(left, right, (((1,), (1,)), ((), ())), preferred_element_type=F32)


def dot(left, right):
    return jnp.dot(left, right, preferred_element_type=F32)


def halves(values):
    upper = values.astype(BF16)
    return upper, (values - upper.astype(F32)).astype(BF16)


def await_bytes(ref, sem):
    pltpu.make_async_copy(ref, ref, sem).wait()


def kernel(
    n_store,
    n_feat,
    features,
    serve_rows,
    row_counts,
    index_one,
    index_two,
    w1_self,
    w1_neigh,
    w2_self,
    w2_neigh,
    out_grad,
    h2,
    out_w1s,
    out_w1n,
    out_w2s,
    out_w2n,
    table,
    stage,
    rows_in,
    owner_of,
    pick,
    both,
    nodes_out,
    nodes_in,
    w1_own,
    w1_all,
    hid_own,
    hid_all,
    self_t,
    count_t,
    back_out,
    back_in,
    slope_own,
    slope_all,
    tiles2,
    tiles2_in,
    sum2,
    sum2_all,
    tiles1,
    tiles1_in,
    sum1,
    sum1_all,
    send_sems,
    recv_sems,
    group_sems,
):
    my_store, my_feat = lax.axis_index("store"), lax.axis_index("feat")
    width, papers = features.shape
    cap = serve_rows.shape[2]
    entries, nodes = index_one.shape[1:]
    fan_one = entries - 1
    fan_two = index_two.shape[1] - 1
    hidden = w2_self.shape[1]
    units = w2_self.shape[0]
    own_rows = nodes // n_feat

    def store_peer(step):
        return lax.rem(my_store + step + n_store, n_store)

    def feat_peer(step):
        return lax.rem(my_feat + step + n_feat, n_feat)

    def send(src, dst, which, recv_sem, axis, peer):
        pltpu.make_async_remote_copy(
            src_ref=src,
            dst_ref=dst,
            send_sem=send_sems.at[which],
            recv_sem=recv_sem,
            device_id={axis: peer},
            device_id_type=MESH,
        ).start()

    def keep(src, dst, sem):
        pltpu.make_async_copy(src, dst, sem).start()

    def each_feat(fn):
        def step(k, carry):
            fn(feat_peer(k))
            return carry

        lax.fori_loop(1, n_feat, step, 0)

    def each_store(fn):
        def step(k, carry):
            fn(store_peer(k))
            return carry

        lax.fori_loop(1, n_store, step, 0)

    barrier = pltpu.get_barrier_semaphore()
    each_store(
        lambda peer: pl.semaphore_signal(barrier, inc=1, device_id={"store": peer}, device_id_type=MESH)
    )
    each_feat(
        lambda peer: pl.semaphore_signal(barrier, inc=1, device_id={"feat": peer}, device_id_type=MESH)
    )

    highs = papers // LOW
    for high in range(highs):
        table[high * width : (high + 1) * width, :] = features[:, high * LOW : (high + 1) * LOW].astype(BF16)
    w1_own[0:width, :] = w1_self[...]
    w1_own[width : 2 * width, :] = w1_neigh[...]
    pad_rows = w1_all.shape[1] - 2 * width
    for group in range(n_feat):
        w1_all[group, 2 * width :, :] = jnp.zeros((pad_rows, hidden), BF16)

    pl.semaphore_wait(barrier, n_store + n_feat - 2)

    low_ids = lax.broadcasted_iota(jnp.int32, (LOW, cap), 0)
    group_size = n_store // group_sems.shape[0]

    def serve(trainer):
        wanted = serve_rows[0, pl.ds(trainer, 1), :]
        low, high_of = wanted & (LOW - 1), wanted // LOW
        one_hot = jnp.where(low_ids == low, 1.0, 0.0).astype(BF16)
        found = dot(table[...], one_hot)
        total = jnp.zeros((width, cap), F32)
        for high in range(highs):
            total += jnp.where(high_of == high, found[high * width : (high + 1) * width, :], 0.0)
        stage[trainer] = total.astype(BF16)

    def serve_and_send(trainer):
        serve(trainer)
        send(stage.at[trainer], rows_in.at[my_store], 0, group_sems.at[my_store // group_size], "store", trainer)

    def send_w1(peer):
        send(w1_own, w1_all.at[my_feat, pl.ds(0, 2 * width)], 1, recv_sems.at[1], "feat", peer)

    def outward(k, carry):
        serve_and_send(store_peer(k))
        serve_and_send(store_peer(-k))
        return carry

    half_store = n_store // 2
    shared = min(half_store, n_feat)

    def outward_both(k, carry):
        outward(k, carry)
        send_w1(feat_peer(k))
        return carry

    lax.fori_loop(1, shared, outward_both, 0)
    lax.fori_loop(shared, half_store, outward, 0)
    for k in range(shared, n_feat):
        send_w1(feat_peer(k))
    serve_and_send(store_peer(half_store))
    serve(my_store)
    keep(stage.at[my_store], rows_in.at[my_store], group_sems.at[my_store // group_size])
    keep(w1_own, w1_all.at[my_feat, pl.ds(0, 2 * width)], recv_sems.at[1])

    raw = index_one[0]
    owners = raw // cap
    place = (raw & (cap - 1)).astype(F32)
    counts = jnp.ones(raw.shape, F32)
    for owner in range(n_store):
        counts = jnp.where(owners == owner, row_counts[0:1, owner : owner + 1].astype(F32), counts)
    place = place - jnp.floor((place + 0.5) / counts) * counts
    owner_of[0:entries, :] = owners
    place = place.astype(jnp.int32)
    slot_ids = lax.broadcasted_iota(jnp.int32, (cap, nodes), 0)
    for entry in range(entries):
        pick[entry] = jnp.where(slot_ids == place[entry : entry + 1, :], 1.0, 0.0).astype(BF16)

    strip = 64
    targets = index_two.shape[2]

    def second_tables(part, carry):
        node_ids = lax.broadcasted_iota(jnp.int32, (strip, targets), 0) + part * strip
        at = pl.ds(pl.multiple_of(part * strip, strip), strip)
        self_t[at, :] = jnp.where(node_ids == index_two[0, 0:1, :], 1.0, 0.0).astype(BF16)
        total = jnp.zeros((strip, targets), F32)
        for entry in range(1, fan_two + 1):
            total += jnp.where(node_ids == index_two[0, entry : entry + 1, :], 1.0, 0.0)
        count_t[at, :] = total.astype(BF16)
        return carry

    lax.fori_loop(0, nodes // strip, second_tables, 0)

    both[...] = jnp.zeros_like(both)

    def gather(entry, group, at):
        found = dot(rows_in[pl.ds(group * group_size, group_size)].reshape(group_size * width, cap), pick[entry])
        of = owner_of[pl.ds(entry, 1), :]
        total = both[at : at + width, :]
        for member in range(group_size):
            total += jnp.where(
                of == group * group_size + member, found[member * width : (member + 1) * width, :], 0.0
            )
        both[at : at + width, :] = total

    for group in range(n_store // group_size):
        await_bytes(rows_in.at[pl.ds(group * group_size, group_size)], group_sems.at[group])
        gather(0, group, 0)

        def neighbours(entry, carry, group=group):
            gather(entry, group, width)
            return carry

        lax.fori_loop(1, entries, neighbours, 0)
    both[width : 2 * width, :] = both[width : 2 * width, :] / fan_one
    node_inputs = both[0 : 2 * width, :].astype(BF16)
    turned = both[...].T.astype(BF16)
    for group in range(n_feat):
        nodes_out[group] = turned[group * own_rows : (group + 1) * own_rows, :]

    each_feat(lambda peer: send(nodes_out.at[peer], nodes_in.at[my_feat], 2, recv_sems.at[2], "feat", peer))
    keep(nodes_out.at[my_feat], nodes_in.at[my_feat], recv_sems.at[2])

    await_bytes(w1_all.at[:, pl.ds(0, 2 * width)], recv_sems.at[1])
    await_bytes(nodes_in, recv_sems.at[2])
    own_nodes = jnp.concatenate([nodes_in[group] for group in range(n_feat)], axis=1)
    pre_one = dot(own_nodes, w1_all[...].reshape(n_feat * w1_all.shape[1], hidden))
    hid_own[...] = (pre_one * jax.nn.sigmoid(pre_one)).astype(BF16)
    each_feat(lambda peer: send(hid_own, hid_all.at[my_feat], 3, recv_sems.at[3], "feat", peer))
    keep(hid_own, hid_all.at[my_feat], recv_sems.at[3])
    slope_one = slope(pre_one)
    await_bytes(hid_all, recv_sems.at[3])

    hid = hid_all[...].reshape(nodes, hidden)
    w2 = jnp.concatenate([w2_self[...], w2_neigh[...]], axis=0)
    mixed = nt_dot(w2, hid)
    upper, lower = halves(mixed)
    self_term = dot(jnp.concatenate([upper[:units], lower[:units]], axis=0), self_t[...])
    neigh_term = dot(jnp.concatenate([upper[units:], lower[units:]], axis=0), count_t[...])
    pre_two = self_term[:units] + self_term[units:] + (neigh_term[:units] + neigh_term[units:]) / fan_two
    h2[...] = (pre_two * jax.nn.sigmoid(pre_two)).astype(BF16)
    grad_two = (out_grad[...].astype(F32) * slope(pre_two)).astype(BF16)
    node_grad = jnp.concatenate([nt_dot(grad_two, self_t[...]), nt_dot(grad_two, count_t[...]) / fan_two], axis=0)
    upper, lower = halves(node_grad.T)
    back = dot(jnp.concatenate([upper, lower], axis=1), jnp.concatenate([w2, w2], axis=0))
    back_out[...] = back.astype(BF16).reshape(n_feat, own_rows, hidden)
    each_feat(lambda peer: send(back_out.at[peer], back_in.at[my_feat], 4, recv_sems.at[4], "feat", peer))
    keep(back_out.at[my_feat], back_in.at[my_feat], recv_sems.at[4])

    upper, lower = halves(node_grad)
    grad_w2 = dot(jnp.concatenate([upper, lower], axis=0), hid)
    grad_w2 = (grad_w2[: 2 * units] + grad_w2[2 * units :]).astype(BF16)
    across = hidden // 128
    for row in range(2 * units // 16):
        for col in range(across):
            tiles2[row * across + col] = grad_w2[row * 16 : (row + 1) * 16, col * 128 : (col + 1) * 128]
    share2 = tiles2.shape[0] // n_store
    each_store(
        lambda peer: send(
            tiles2.at[pl.ds(peer * share2, share2)], tiles2_in.at[my_store], 5, recv_sems.at[5], "store", peer
        )
    )
    keep(tiles2.at[pl.ds(my_store * share2, share2)], tiles2_in.at[my_store], recv_sems.at[5])

    await_bytes(back_in, recv_sems.at[4])
    total = back_in[0].astype(F32)
    for group in range(1, n_feat):
        total += back_in[group].astype(F32)
    slope_own[...] = (total * slope_one).astype(BF16)
    each_feat(lambda peer: send(slope_own, slope_all.at[my_feat], 6, recv_sems.at[6], "feat", peer))
    keep(slope_own, slope_all.at[my_feat], recv_sems.at[6])

    await_bytes(tiles2_in, recv_sems.at[5])
    total = tiles2_in[0].astype(F32)
    for store in range(1, n_store):
        total += tiles2_in[store].astype(F32)
    sum2[...] = total.astype(BF16)
    each_store(
        lambda peer: send(sum2, sum2_all.at[pl.ds(my_store * share2, share2)], 7, recv_sems.at[7], "store", peer)
    )
    keep(sum2, sum2_all.at[pl.ds(my_store * share2, share2)], recv_sems.at[7])

    await_bytes(slope_all, recv_sems.at[6])
    grad_w1 = dot(node_inputs, slope_all[...].reshape(nodes, hidden)).astype(BF16)
    for row in range(2 * width // 16):
        for col in range(across):
            tiles1[row * across + col] = grad_w1[row * 16 : (row + 1) * 16, col * 128 : (col + 1) * 128]
    share1 = sum1.shape[0]
    summers = tiles1.shape[0] // share1

    def send_tiles1(peer):
        @pl.when(peer < summers)
        def _():
            send(tiles1.at[pl.ds(peer * share1, share1)], tiles1_in.at[my_store], 8, recv_sems.at[8], "store", peer)

    each_store(send_tiles1)

    await_bytes(sum2_all, recv_sems.at[7])
    for row in range(2 * units // 16):
        out, at = (out_w2s, row * 16) if row * 16 < units else (out_w2n, row * 16 - units)
        for col in range(across):
            out[at : at + 16, col * 128 : (col + 1) * 128] = sum2_all[row * across + col].astype(F32)

    @pl.when(my_store < summers)
    def _():
        keep(tiles1.at[pl.ds(my_store * share1, share1)], tiles1_in.at[my_store], recv_sems.at[8])
        await_bytes(tiles1_in, recv_sems.at[8])
        total = tiles1_in[0].astype(F32)
        for store in range(1, n_store):
            total += tiles1_in[store].astype(F32)
        sum1[...] = total.astype(BF16)
        each_store(
            lambda peer: send(sum1, sum1_all.at[pl.ds(my_store * share1, share1)], 9, recv_sems.at[9], "store", peer)
        )
        keep(sum1, sum1_all.at[pl.ds(my_store * share1, share1)], recv_sems.at[9])

    await_bytes(sum1_all, recv_sems.at[9])
    for row in range(2 * width // 16):
        out, at = (out_w1s, row * 16) if row * 16 < width else (out_w1n, row * 16 - width)
        for col in range(across):
            out[at : at + 16, col * 128 : (col + 1) * 128] = sum1_all[row * across + col].astype(F32)

    await_bytes(stage.at[pl.ds(0, n_store - 1)], send_sems.at[0])
    await_bytes(w1_all.at[pl.ds(0, n_feat - 1), pl.ds(0, 2 * width)], send_sems.at[1])
    await_bytes(nodes_out.at[pl.ds(0, n_feat - 1)], send_sems.at[2])
    await_bytes(hid_all.at[pl.ds(0, n_feat - 1)], send_sems.at[3])
    await_bytes(back_out.at[pl.ds(0, n_feat - 1)], send_sems.at[4])
    await_bytes(tiles2.at[pl.ds(0, (n_store - 1) * share2)], send_sems.at[5])
    await_bytes(slope_all.at[pl.ds(0, n_feat - 1)], send_sems.at[6])
    await_bytes(sum2_all.at[pl.ds(0, (n_store - 1) * share2)], send_sems.at[7])
    await_bytes(tiles1.at[pl.ds(0, (summers - 1) * share1)], send_sems.at[8])

    @pl.when(my_store >= summers)
    def _():
        await_bytes(tiles1.at[pl.ds(0, share1)], send_sems.at[8])

    @pl.when(my_store < summers)
    def _():
        await_bytes(tiles1_in.at[pl.ds(0, n_store - 1)], send_sems.at[9])


def body(n_store, n_feat, *args):
    features, serve_rows, _, index_one, index_two, w1_self, _, w2_self, _, out_grad = args
    width, papers = features.shape
    cap = serve_rows.shape[2]
    entries, nodes = index_one.shape[1:]
    targets = index_two.shape[2]
    hidden, units = w2_self.shape[1], w2_self.shape[0]
    own_rows = nodes // n_feat
    padded = -(-2 * width // 128) * 128
    tiles2 = 2 * units // 16 * (hidden // 128)
    tiles1 = 2 * width // 16 * (hidden // 128)
    share2 = tiles2 // n_store
    share1 = -(-tiles1 // n_store)
    groups = 4
    scratch = [
        pltpu.VMEM((papers // LOW * width, LOW), BF16),
        pltpu.VMEM((n_store, width, cap), BF16),
        pltpu.VMEM((n_store, width, cap), BF16),
        pltpu.VMEM((entries, nodes), jnp.int32),
        pltpu.VMEM((entries, cap, nodes), BF16),
        pltpu.VMEM((padded, nodes), F32),
        pltpu.VMEM((n_feat, own_rows, padded), BF16),
        pltpu.VMEM((n_feat, own_rows, padded), BF16),
        pltpu.VMEM((2 * width, hidden), BF16),
        pltpu.VMEM((n_feat, padded, hidden), BF16),
        pltpu.VMEM((own_rows, hidden), BF16),
        pltpu.VMEM((n_feat, own_rows, hidden), BF16),
        pltpu.VMEM((nodes, targets), BF16),
        pltpu.VMEM((nodes, targets), BF16),
        pltpu.VMEM((n_feat, own_rows, hidden), BF16),
        pltpu.VMEM((n_feat, own_rows, hidden), BF16),
        pltpu.VMEM((own_rows, hidden), BF16),
        pltpu.VMEM((n_feat, own_rows, hidden), BF16),
        pltpu.VMEM((tiles2, 16, 128), BF16),
        pltpu.VMEM((n_store, share2, 16, 128), BF16),
        pltpu.VMEM((share2, 16, 128), BF16),
        pltpu.VMEM((tiles2, 16, 128), BF16),
        pltpu.VMEM((tiles1, 16, 128), BF16),
        pltpu.VMEM((n_store, share1, 16, 128), BF16),
        pltpu.VMEM((share1, 16, 128), BF16),
        pltpu.VMEM((tiles1, 16, 128), BF16),
        pltpu.SemaphoreType.DMA((10,)),
        pltpu.SemaphoreType.DMA((10,)),
        pltpu.SemaphoreType.DMA((groups,)),
    ]
    return pl.pallas_call(
        functools.partial(kernel, n_store, n_feat),
        out_shape=[
            jax.ShapeDtypeStruct((units, targets), BF16),
            jax.ShapeDtypeStruct((width, hidden), F32),
            jax.ShapeDtypeStruct((width, hidden), F32),
            jax.ShapeDtypeStruct((units, hidden), F32),
            jax.ShapeDtypeStruct((units, hidden), F32),
        ],
        in_specs=[pl.BlockSpec(memory_space=pltpu.VMEM)] * len(args),
        out_specs=[pl.BlockSpec(memory_space=pltpu.VMEM)] * 5,
        scratch_shapes=scratch,
        compiler_params=pltpu.CompilerParams(
            collective_id=0, has_side_effects=True, vmem_limit_bytes=48 * 1024 * 1024
        ),
    )(*args)


def solution(mesh):
    return jax.shard_map(
        functools.partial(body, mesh.shape["store"], mesh.shape["feat"]),
        mesh=mesh,
        in_specs=(
            P("feat", "store"),
            P("store", None, None),
            P("store", None),
            P("store", None, None),
            P("store", None, None),
            P("feat", None),
            P("feat", None),
            P("feat", None),
            P("feat", None),
            P("feat", "store"),
        ),
        out_specs=(
            P("feat", "store"),
            P("feat", None),
            P("feat", None),
            P("feat", None),
            P("feat", None),
        ),
        check_vma=False,
    )
```

time: 632 us -> 164 us (0.26)
  the two profiles are of different devices: /device:TPU:1 before, /device:TPU:7 now
where the time goes in v1:
time: 164 us
  Pallas kernels  153 us (93%)
  local copies, waits for them, and re-layouts  10.5 us (6%)
    pallas_call x1, Pallas kernels, body(): pl.pallas_call(functools.partial(kernel, n_store, n_feat), out_shape=[jax...  153 us
    unnamed x24, local copies, waits for them, and re-layouts  10.5 us

profile of v1, /device:TPU:7, one launch (start us, length us, event | category | flops | bytes accessed | tf_op | source)
XLA Modules:
  0.0 163.8 jit_solution(17826199157171596325)
XLA Ops:
  0.6 0.0 copy-start.8
  0.6 0.0 copy-start.6
  0.7 0.7 copy.15.index_one
  1.4 0.0 copy-done.8
  1.4 0.0 copy-done.6
  1.4 0.0 copy-start
  1.4 1.1 copy-done
  2.5 0.0 copy-start.1
  2.5 0.9 copy-done.1
  3.4 0.0 copy-start.2
  3.4 0.9 copy-done.2
  4.4 0.0 copy-start.3
  4.4 0.9 copy-done.3
  5.2 0.0 copy-start.4
  5.2 0.9 copy-done.4
  6.1 0.0 copy-start.5
  6.1 0.8 copy-done.5
  7.0 0.0 copy-start.7
  7.0 0.8 copy-done.7
  7.7 152.7 %shard_map.137 = (bf16[64,512]{1,0:T(8,128)(2,1)S(1)}, f32[48,1024]{1,0:T(8,128)S(1)}, f32[48,1024]{1,0:T(8,128)S(1)}, f32[64,1024]{1,0:T(8,128)S(1)}, f32[64,1024]{1,0:T(8,128)S(1)}) custom-call(f32[48,4096]{1,0:T(8,128)S(1)} %copy-done, s32[1,32,256]{2,1,0:T(8,128)S(1)} %copy-done.6, s32[1,32]{1,0:T(1,128)S(1)} %copy-done.8, ...), custom_call_target="tpu_custom_call" | custom-call | tf_op jit(solution)/shard_map/pallas_call | solution.py:411
  160.4 0.6 copy.21
  161.0 0.7 copy.22
  161.7 0.7 copy.23
  162.4 0.7 copy.24
  163.1 0.7 copy.25
Async XLA Ops:
  0.6 0.8 copy-start.8
  0.6 0.8 copy-start.6
  1.4 1.1 copy-start
  2.5 0.9 copy-start.1
  3.4 0.9 copy-start.2
  4.4 0.9 copy-start.3
  5.2 0.9 copy-start.4
  6.1 0.8 copy-start.5
  7.0 0.8 copy-start.7

commit v2 on v1

v2 whole, which is shorter than its diff:
```python
import functools

import jax
import jax.numpy as jnp
from jax import lax
from jax.experimental import pallas as pl
from jax.experimental.pallas import tpu as pltpu
from jax.sharding import PartitionSpec as P

MESH = pl.DeviceIdType.MESH
F32 = jnp.float32
BF16 = jnp.bfloat16
LOW = 256


def slope(values):
    sig = jax.nn.sigmoid(values)
    return sig * (1.0 + values * (1.0 - sig))


def nt_dot(left, right):
    return lax.dot_general(left, right, (((1,), (1,)), ((), ())), preferred_element_type=F32)


def dot(left, right):
    return jnp.dot(left, right, preferred_element_type=F32)


def halves(values):
    upper = values.astype(BF16)
    return upper, (values - upper.astype(F32)).astype(BF16)


def await_bytes(ref, sem):
    pltpu.make_async_copy(ref, ref, sem).wait()


SENDS = ("rows", "w1", "w1_swap", "nodes", "hid0", "hid1", "back0", "back1", "slope0", "slope1") + tuple(
    total + stage for total in ("w2", "w1_0", "w1_1") for stage in ("_merge", "_reduce", "_spread", "_swap")
)
INPUTS = 10
GROUPS = 8
HALVES = 2


def kernel(
    n_store,
    n_feat,
    features_hbm,
    serve_rows_hbm,
    row_counts_hbm,
    index_one_hbm,
    index_two_hbm,
    w1_self_hbm,
    w1_neigh_hbm,
    w2_self_hbm,
    w2_neigh_hbm,
    out_grad_hbm,
    h2,
    out_w1s,
    out_w1n,
    out_w2s,
    out_w2n,
    features,
    serve_rows,
    row_counts,
    index_one,
    index_two,
    w2,
    out_grad,
    table,
    stage,
    rows_in,
    owner_of,
    pick,
    both,
    nodes_out,
    nodes_in,
    w1_own,
    w1_all,
    hid_own,
    hid_all,
    self_t,
    count_t,
    back_out,
    back_in,
    slope_own,
    slope_all,
    w2_total,
    w1_total_0,
    w1_total_1,
    input_sems,
    send_sems,
    recv_sems,
    group_sems,
):
    my_store, my_feat = lax.axis_index("store"), lax.axis_index("feat")
    my_chip, my_core = my_store // 2, lax.rem(my_store, 2)
    n_chip = n_store // 2
    width, papers = features.shape
    cap = serve_rows.shape[2]
    entries, nodes = index_one.shape[1:]
    fan_one = entries - 1
    fan_two = index_two.shape[1] - 1
    units, hidden = w2.shape[0] // 2, w2.shape[1]
    columns = hidden // HALVES
    own_rows = nodes // n_feat
    pad = both.shape[0] // 2
    pending = []

    def store_peer(step):
        return lax.rem(my_store + step + n_store, n_store)

    def feat_peer(step):
        return lax.rem(my_feat + step + n_feat, n_feat)

    def chip_peer(step):
        return lax.rem(my_chip + step + n_chip, n_chip)

    def send(src, dst, name, recv_sem, axis, peer):
        pltpu.make_async_remote_copy(
            src_ref=src,
            dst_ref=dst,
            send_sem=send_sems.at[SENDS.index(name)],
            recv_sem=recv_sem,
            device_id={axis: peer},
            device_id_type=MESH,
        ).start()

    def recv_of(name):
        return recv_sems.at[SENDS.index(name)]

    def later(ref, name):
        pending.append(lambda: await_bytes(ref, send_sems.at[SENDS.index(name)]))

    def keep(src, dst, sem):
        pltpu.make_async_copy(src, dst, sem).start()

    def loop(low, high, fn):
        def step(k, carry):
            fn(k)
            return carry

        lax.fori_loop(low, high, step, 0)

    def share(src_of, dst, name):
        loop(1, n_feat, lambda k: send(src_of(feat_peer(k)), dst, name, recv_of(name), "feat", feat_peer(k)))
        keep(src_of(my_feat), dst, recv_of(name))

    barrier = pltpu.get_barrier_semaphore()

    def greet(axis, peer):
        pl.semaphore_signal(barrier, inc=1, device_id={axis: peer}, device_id_type=MESH)

    reads = (
        (features_hbm, features),
        (serve_rows_hbm, serve_rows),
        (w1_self_hbm, w1_own.at[0]),
        (w1_neigh_hbm, w1_own.at[1]),
        (row_counts_hbm, row_counts),
        (index_one_hbm, index_one),
        (index_two_hbm, index_two),
        (w2_self_hbm, w2.at[pl.ds(0, units)]),
        (w2_neigh_hbm, w2.at[pl.ds(units, units)]),
        (out_grad_hbm, out_grad),
    )
    reads = [pltpu.make_async_copy(src, dst, input_sems.at[i]) for i, (src, dst) in enumerate(reads)]
    for read in reads:
        read.start()
    loop(1, n_store, lambda k: greet("store", store_peer(k)))
    loop(1, n_feat, lambda k: greet("feat", feat_peer(k)))
    for group in range(n_feat):
        for half in range(2):
            w1_all[group, half, width:, :] = jnp.zeros((pad - width, hidden), BF16)
    both[...] = jnp.zeros_like(both)

    reads[0].wait()
    reads[1].wait()
    highs = papers // LOW
    for high in range(highs):
        table[high * width : (high + 1) * width, :] = features[:, high * LOW : (high + 1) * LOW].astype(BF16)
    low_ids = lax.broadcasted_iota(jnp.int32, (LOW, cap), 0)

    def serve(trainer):
        wanted = serve_rows[0, pl.ds(trainer, 1), :]
        low, high_of = wanted & (LOW - 1), wanted // LOW
        one_hot = jnp.where(low_ids == low, 1.0, 0.0).astype(BF16)
        found = dot(table[...], one_hot)
        total = jnp.zeros((width, cap), F32)
        for high in range(highs):
            total += jnp.where(high_of == high, found[high * width : (high + 1) * width, :], 0.0)
        stage[trainer] = total.astype(BF16)

    loop(0, n_store, serve)
    for read in reads[2:]:
        read.wait()
    pl.semaphore_wait(barrier, n_store + n_feat - 2)

    half_store = n_store // 2
    group_size = n_store // GROUPS

    def send_rows(trainer, rank):
        send(stage.at[trainer], rows_in.at[rank], "rows", group_sems.at[rank // group_size], "store", trainer)

    def send_w1(peer):
        send(w1_own.at[my_core], w1_all.at[my_feat, my_core, pl.ds(0, width)], "w1", recv_of("w1"), "feat", peer)

    def send_pair(i):
        send_rows(store_peer(half_store - i), 2 * i - 1)
        send_rows(store_peer(i - half_store), 2 * i)

    def send_pair_and_w1(i):
        send_pair(i)
        send_w1(feat_peer(i))

    send_rows(store_peer(half_store), 0)
    shared = min(half_store, n_feat)
    loop(1, shared, send_pair_and_w1)
    loop(shared, half_store, send_pair)
    loop(shared, n_feat, lambda i: send_w1(feat_peer(i)))
    keep(stage.at[my_store], rows_in.at[n_store - 1], group_sems.at[GROUPS - 1])
    keep(w1_own.at[my_core], w1_all.at[my_feat, my_core, pl.ds(0, width)], recv_of("w1"))
    later(stage.at[pl.ds(0, n_store - 1)], "rows")
    later(w1_all.at[pl.ds(0, n_feat - 1), 0, pl.ds(0, width)], "w1")

    raw = index_one[0]
    owners = raw // cap
    place = (raw & (cap - 1)).astype(F32)
    counts = jnp.ones(raw.shape, F32)
    for owner in range(n_store):
        counts = jnp.where(owners == owner, row_counts[0:1, owner : owner + 1].astype(F32), counts)
    place = place - jnp.floor((place + 0.5) / counts) * counts
    owner_of[0:entries, :] = owners
    place = place.astype(jnp.int32)
    slot_ids = lax.broadcasted_iota(jnp.int32, (cap, nodes), 0)
    for entry in range(entries):
        pick[entry] = jnp.where(slot_ids == place[entry : entry + 1, :], 1.0, 0.0).astype(BF16)

    strip = 64
    targets = index_two.shape[2]

    def second_tables(part):
        node_ids = lax.broadcasted_iota(jnp.int32, (strip, targets), 0) + part * strip
        at = pl.ds(pl.multiple_of(part * strip, strip), strip)
        self_t[at, :] = jnp.where(node_ids == index_two[0, 0:1, :], 1.0, 0.0).astype(BF16)
        total = jnp.zeros((strip, targets), F32)
        for entry in range(1, fan_two + 1):
            total += jnp.where(node_ids == index_two[0, entry : entry + 1, :], 1.0, 0.0)
        count_t[at, :] = total.astype(BF16)

    loop(0, nodes // strip, second_tables)

    def gather(entry, group, at):
        found = dot(rows_in[pl.ds(group * group_size, group_size)].reshape(group_size * width, cap), pick[entry])
        of = owner_of[pl.ds(entry, 1), :]
        total = both[at : at + width, :]
        for member in range(group_size):
            rank = group * group_size + member
            offset = half_store - (rank + 1) // 2 if rank % 2 else rank // 2 - half_store
            total += jnp.where(of == store_peer(-offset), found[member * width : (member + 1) * width, :], 0.0)
        both[at : at + width, :] = total

    for group in range(GROUPS):
        await_bytes(rows_in.at[pl.ds(group * group_size, group_size)], group_sems.at[group])
        gather(0, group, 0)
        loop(1, entries, lambda entry, group=group: gather(entry, group, pad))
        if group == GROUPS - 3:
            await_bytes(w1_all.at[:, 0, pl.ds(0, width)], recv_of("w1"))
            mine = w1_all.at[:, my_core, pl.ds(0, width)]
            send(mine, mine, "w1_swap", recv_of("w1_swap"), "store", my_store + 1 - 2 * my_core)
            later(w1_all.at[:, 0, pl.ds(0, width)], "w1_swap")
    both[pad : pad + width, :] = both[pad : pad + width, :] / fan_one
    node_inputs = both[...].astype(BF16)
    turned = both[...].T.astype(BF16)
    for group in range(n_feat):
        nodes_out[group] = turned[group * own_rows : (group + 1) * own_rows, :]

    share(lambda peer: nodes_out.at[peer], nodes_in.at[my_feat], "nodes")
    later(nodes_out.at[pl.ds(0, n_feat - 1)], "nodes")

    await_bytes(w1_all.at[:, 0, pl.ds(0, width)], recv_of("w1_swap"))
    await_bytes(nodes_in, recv_of("nodes"))
    own_nodes = jnp.concatenate([nodes_in[group] for group in range(n_feat)], axis=1)
    slope_one = []
    for half in range(HALVES):
        cols = slice(half * columns, (half + 1) * columns)
        pre_one = dot(own_nodes, w1_all[:, :, :, cols].reshape(n_feat * 2 * pad, columns))
        hid_own[half] = (pre_one * jax.nn.sigmoid(pre_one)).astype(BF16)
        name = f"hid{half}"
        share(lambda peer, half=half: hid_own.at[half], hid_all.at[half, my_feat], name)
        later(hid_all.at[half, pl.ds(0, n_feat - 1)], name)
        slope_one.append(slope(pre_one))

    mixed = jnp.zeros((2 * units, nodes), F32)
    hid = []
    for half in range(HALVES):
        await_bytes(hid_all.at[half], recv_of(f"hid{half}"))
        hid.append(hid_all[half].reshape(nodes, columns))
        mixed += nt_dot(w2[:, half * columns : (half + 1) * columns], hid[half])
    upper, lower = halves(mixed)
    self_term = dot(jnp.concatenate([upper[:units], lower[:units]], axis=0), self_t[...])
    neigh_term = dot(jnp.concatenate([upper[units:], lower[units:]], axis=0), count_t[...])
    pre_two = self_term[:units] + self_term[units:] + (neigh_term[:units] + neigh_term[units:]) / fan_two
    grad_two = (out_grad[...].astype(F32) * slope(pre_two)).astype(BF16)
    node_grad = jnp.concatenate([nt_dot(grad_two, self_t[...]), nt_dot(grad_two, count_t[...]) / fan_two], axis=0)
    upper, lower = halves(node_grad.T)
    turned = jnp.concatenate([upper, lower], axis=1)
    for half in range(HALVES):
        weights = w2[:, half * columns : (half + 1) * columns]
        back = dot(turned, jnp.concatenate([weights, weights], axis=0))
        back_out[half] = back.astype(BF16).reshape(n_feat, own_rows, columns)
        name = f"back{half}"
        share(lambda peer, half=half: back_out.at[half, peer], back_in.at[half, my_feat], name)
        later(back_out.at[half, pl.ds(0, n_feat - 1)], name)
    h2[...] = (pre_two * jax.nn.sigmoid(pre_two)).astype(BF16)

    sibling = my_store + 1 - 2 * my_core

    def total_of(ref, name):
        tiles = ref.shape[1] // 2
        per = -(-tiles // n_chip)
        summers = tiles // per
        spread = summers * 4 == n_chip * 3

        def sums(chip):
            return lax.rem(chip, 4) != 3 if spread else chip < summers

        def first(chip):
            return (chip - chip // 4 if spread else chip) * per

        part, merged = ref.at[0], ref.at[1]
        arrived, total = ref.at[2], ref.at[3]

        def fill(half, grad, row0=0):
            across = grad.shape[1] // 128
            for row in range(grad.shape[0] // 16):
                for col in range(across):
                    part[half * tiles + row * across + col] = grad[
                        row * 16 : (row + 1) * 16, col * 128 : (col + 1) * 128
                    ]

        def merge():
            own = pl.ds((1 - my_core) * tiles, tiles)
            send(part.at[own], merged.at[pl.ds(0, tiles)], name + "_merge", recv_of(name + "_merge"), "store", sibling)
            later(part.at[pl.ds(0, tiles)], name + "_merge")

        def reduce():
            await_bytes(merged.at[pl.ds(0, tiles)], recv_of(name + "_merge"))
            both_cores = part[pl.ds(my_core * tiles, tiles)].astype(F32) + merged[0:tiles].astype(F32)
            merged[tiles : 2 * tiles] = both_cores.astype(BF16)

            def to(k):
                chip = chip_peer(k)

                @pl.when(sums(chip))
                def _():
                    send(
                        merged.at[pl.ds(tiles + first(chip), per)],
                        arrived.at[pl.ds(my_chip * per, per)],
                        name + "_reduce",
                        recv_of(name + "_reduce"),
                        "store",
                        chip * 2 + my_core,
                    )

            loop(1, n_chip, to)

            def sent():
                for count, wait_here in ((summers - 1, sums(my_chip)), (summers, jnp.logical_not(sums(my_chip)))):
                    if summers == n_chip and count == n_chip:
                        continue

                    @pl.when(wait_here)
                    def _(count=count):
                        await_bytes(merged.at[pl.ds(0, count * per)], send_sems.at[SENDS.index(name + "_reduce")])

            pending.append(sent)

        def spread_out():
            @pl.when(sums(my_chip))
            def _():
                mine = pl.ds(first(my_chip), per)
                keep(
                    merged.at[pl.ds(tiles + first(my_chip), per)],
                    arrived.at[pl.ds(my_chip * per, per)],
                    recv_of(name + "_reduce"),
                )
                await_bytes(arrived.at[pl.ds(0, n_chip * per)], recv_of(name + "_reduce"))
                summed = arrived[0:per].astype(F32)
                for chip in range(1, n_chip):
                    summed += arrived[chip * per : (chip + 1) * per].astype(F32)
                at = pl.ds(my_core * tiles + first(my_chip), per)
                total[at] = summed.astype(BF16)
                loop(
                    1,
                    n_chip,
                    lambda k: send(
                        total.at[at],
                        total.at[at],
                        name + "_spread",
                        recv_of(name + "_spread"),
                        "store",
                        chip_peer(k) * 2 + my_core,
                    ),
                )

            def sent():
                @pl.when(sums(my_chip))
                def _():
                    await_bytes(arrived.at[pl.ds(0, (n_chip - 1) * per)], send_sems.at[SENDS.index(name + "_spread")])

            pending.append(sent)

        def swap():
            for count, wait_here in ((summers - 1, sums(my_chip)), (summers, jnp.logical_not(sums(my_chip)))):
                if summers == n_chip and count == n_chip:
                    continue

                @pl.when(wait_here)
                def _(count=count):
                    await_bytes(total.at[pl.ds(0, count * per)], recv_of(name + "_spread"))

            mine = total.at[pl.ds(my_core * tiles, tiles)]
            send(mine, mine, name + "_swap", recv_of(name + "_swap"), "store", sibling)
            later(total.at[pl.ds(0, tiles)], name + "_swap")

        def write(outs, col0, cols, rows):
            await_bytes(total.at[pl.ds(0, tiles)], recv_of(name + "_swap"))
            across = cols // 128
            for half, out in enumerate(outs):
                for row in range(rows // 16):
                    for col in range(across):
                        out[row * 16 : (row + 1) * 16, col0 + col * 128 : col0 + (col + 1) * 128] = total[
                            half * tiles + row * across + col
                        ].astype(F32)

        return fill, merge, reduce, spread_out, swap, write

    fill, merge, reduce2, spread2, swap2, write2 = total_of(w2_total, "w2")
    upper, lower = halves(node_grad)
    stacked = jnp.concatenate([upper, lower], axis=0)
    grad_w2 = jnp.concatenate([dot(stacked, part) for part in hid], axis=1)
    grad_w2 = (grad_w2[: 2 * units] + grad_w2[2 * units :]).astype(BF16)
    fill(0, grad_w2[:units])
    fill(1, grad_w2[units:])
    merge()
    reduce2()

    for half in range(HALVES):
        name = f"back{half}"
        await_bytes(back_in.at[half], recv_of(name))
        total = back_in[half, 0].astype(F32)
        for group in range(1, n_feat):
            total += back_in[half, group].astype(F32)
        slope_own[half] = (total * slope_one[half]).astype(BF16)
        name = f"slope{half}"
        share(lambda peer, half=half: slope_own.at[half], slope_all.at[half, my_feat], name)
        later(slope_all.at[half, pl.ds(0, n_feat - 1)], name)
    spread2()

    steps = []
    for half, ref in enumerate((w1_total_0, w1_total_1)):
        await_bytes(slope_all.at[half], recv_of(f"slope{half}"))
        grad_w1 = dot(node_inputs, slope_all[half].reshape(nodes, columns)).astype(BF16)
        fill, merge, *rest = total_of(ref, f"w1_{half}")
        steps.append(rest)
        fill(0, grad_w1[0:width])
        fill(1, grad_w1[pad : pad + width])
        merge()
        rest[0]()
    swap2()
    steps[0][1]()
    steps[1][1]()
    write2((out_w2s, out_w2n), 0, hidden, units)
    steps[0][2]()
    steps[1][2]()
    steps[0][3]((out_w1s, out_w1n), 0, columns, width)
    steps[1][3]((out_w1s, out_w1n), columns, columns, width)

    for wait in pending:
        wait()


def body(n_store, n_feat, *args):
    features, serve_rows, _, index_one, index_two, w1_self, _, w2_self, _, out_grad = args
    width, papers = features.shape
    cap = serve_rows.shape[2]
    entries, nodes = index_one.shape[1:]
    targets = index_two.shape[2]
    hidden, units = w2_self.shape[1], w2_self.shape[0]
    own_rows = nodes // n_feat
    pad = -(-width // 64) * 64
    columns = hidden // HALVES
    blocks = (HALVES, n_feat, own_rows, columns)
    tiles2 = units // 16 * (hidden // 128)
    tiles1 = width // 16 * (columns // 128)

    def total_scratch(tiles):
        per = -(-tiles // (n_store // 2))
        return pltpu.VMEM((4, max(2 * tiles, n_store // 2 * per), 16, 128), BF16)

    scratch = [
        pltpu.VMEM(features.shape, F32),
        pltpu.VMEM(serve_rows.shape, jnp.int32),
        pltpu.VMEM(args[2].shape, jnp.int32),
        pltpu.VMEM(index_one.shape, jnp.int32),
        pltpu.VMEM(index_two.shape, jnp.int32),
        pltpu.VMEM((2 * units, hidden), BF16),
        pltpu.VMEM(out_grad.shape, BF16),
        pltpu.VMEM((papers // LOW * width, LOW), BF16),
        pltpu.VMEM((n_store, width, cap), BF16),
        pltpu.VMEM((n_store, width, cap), BF16),
        pltpu.VMEM((entries, nodes), jnp.int32),
        pltpu.VMEM((entries, cap, nodes), BF16),
        pltpu.VMEM((2 * pad, nodes), F32),
        pltpu.VMEM((n_feat, own_rows, 2 * pad), BF16),
        pltpu.VMEM((n_feat, own_rows, 2 * pad), BF16),
        pltpu.VMEM((2, width, hidden), BF16),
        pltpu.VMEM((n_feat, 2, pad, hidden), BF16),
        pltpu.VMEM((HALVES, own_rows, columns), BF16),
        pltpu.VMEM(blocks, BF16),
        pltpu.VMEM((nodes, targets), BF16),
        pltpu.VMEM((nodes, targets), BF16),
        pltpu.VMEM(blocks, BF16),
        pltpu.VMEM(blocks, BF16),
        pltpu.VMEM((HALVES, own_rows, columns), BF16),
        pltpu.VMEM(blocks, BF16),
        total_scratch(tiles2),
        total_scratch(tiles1),
        total_scratch(tiles1),
        pltpu.SemaphoreType.DMA((INPUTS,)),
        pltpu.SemaphoreType.DMA((len(SENDS),)),
        pltpu.SemaphoreType.DMA((len(SENDS),)),
        pltpu.SemaphoreType.DMA((GROUPS,)),
    ]
    return pl.pallas_call(
        functools.partial(kernel, n_store, n_feat),
        out_shape=[
            jax.ShapeDtypeStruct((units, targets), BF16),
            jax.ShapeDtypeStruct((width, hidden), F32),
            jax.ShapeDtypeStruct((width, hidden), F32),
            jax.ShapeDtypeStruct((units, hidden), F32),
            jax.ShapeDtypeStruct((units, hidden), F32),
        ],
        in_specs=[pl.BlockSpec(memory_space=pl.ANY)] * len(args),
        out_specs=[pl.BlockSpec(memory_space=pltpu.VMEM)] * 5,
        scratch_shapes=scratch,
        compiler_params=pltpu.CompilerParams(
            collective_id=0, has_side_effects=True, vmem_limit_bytes=48 * 1024 * 1024
        ),
    )(*args)


def solution(mesh):
    return jax.shard_map(
        functools.partial(body, mesh.shape["store"], mesh.shape["feat"]),
        mesh=mesh,
        in_specs=(
            P("feat", "store"),
            P("store", None, None),
            P("store", None),
            P("store", None, None),
            P("store", None, None),
            P("feat", None),
            P("feat", None),
            P("feat", None),
            P("feat", None),
            P("feat", "store"),
        ),
        out_specs=(
            P("feat", "store"),
            P("feat", None),
            P("feat", None),
            P("feat", None),
            P("feat", None),
        ),
        check_vma=False,
    )
```

time: 164 us -> 139 us (0.85)
  the two profiles are of different devices: /device:TPU:7 before, /device:TPU:1 now
where the time goes in v2:
time: 139 us
  Pallas kernels  127 us (91%)
  local copies, waits for them, and re-layouts  10.5 us (8%)
    pallas_call x1, Pallas kernels, body(): pl.pallas_call(functools.partial(kernel, n_store, n_feat), out_shape=[jax...  127 us
    unnamed x24, local copies, waits for them, and re-layouts  10.5 us

profile of v2, /device:TPU:1, one launch (start us, length us, event | category | flops | bytes accessed | tf_op | source)
XLA Modules:
  0.0 138.6 jit_solution(12929916184724071243)
XLA Ops:
  0.6 0.0 copy-start.8
  0.6 0.0 copy-start.6
  0.7 0.7 copy.15.index_one_hbm
  1.4 0.0 copy-done.8
  1.4 0.0 copy-done.6
  1.4 0.0 copy-start
  1.4 1.1 copy-done
  2.5 0.0 copy-start.1
  2.5 0.9 copy-done.1
  3.4 0.0 copy-start.2
  3.4 0.9 copy-done.2
  4.4 0.0 copy-start.3
  4.4 0.9 copy-done.3
  5.2 0.0 copy-start.4
  5.2 0.9 copy-done.4
  6.1 0.0 copy-start.5
  6.1 0.8 copy-done.5
  7.0 0.0 copy-start.7
  7.0 0.8 copy-done.7
  7.7 127.4 %shard_map.137 = (bf16[64,512]{1,0:T(8,128)(2,1)S(1)}, f32[48,1024]{1,0:T(8,128)S(1)}, f32[48,1024]{1,0:T(8,128)S(1)}, f32[64,1024]{1,0:T(8,128)S(1)}, f32[64,1024]{1,0:T(8,128)S(1)}) custom-call(f32[48,4096]{1,0:T(8,128)S(1)} %copy-done, s32[1,32,256]{2,1,0:T(8,128)S(1)} %copy-done.6, s32[1,32]{1,0:T(1,128)S(1)} %copy-done.8, ...), custom_call_target="tpu_custom_call" | custom-call | tf_op jit(solution)/shard_map/pallas_call | solution.py:536
  135.2 0.6 copy.21
  135.8 0.7 copy.22
  136.5 0.7 copy.23
  137.2 0.7 copy.24
  137.9 0.7 copy.25
Async XLA Ops:
  0.6 0.8 copy-start.8
  0.6 0.8 copy-start.6
  1.4 1.1 copy-start
  2.5 0.9 copy-start.1
  3.4 0.9 copy-start.2
  4.4 0.9 copy-start.3
  5.2 0.9 copy-start.4
  6.1 0.8 copy-start.5
  7.0 0.8 copy-start.7

commit v3 on v2

--- a/solution.py
+++ b/solution.py
@@ -35,12 +35,15 @@
     pltpu.make_async_copy(ref, ref, sem).wait()
 
 
-SENDS = ("rows", "w1", "w1_swap", "nodes", "hid0", "hid1", "back0", "back1", "slope0", "slope1") + tuple(
-    total + stage for total in ("w2", "w1_0", "w1_1") for stage in ("_merge", "_reduce", "_spread", "_swap")
+SENDS = (
+    ("rows", "w1", "w1_swap", "nodes")
+    + tuple(what + half + step for what in ("hid", "back", "slope") for half in "01" for step in ("_near", "_far"))
+    + tuple(total + step for total in ("w2", "w1_0", "w1_1") for step in ("_merge", "_reduce", "_spread", "_swap"))
 )
 INPUTS = 10
 GROUPS = 8
 HALVES = 2
+VMEM_LIMIT = 60 * 1024 * 1024
 
 
 def kernel(
@@ -57,13 +60,13 @@
     w2_neigh_hbm,
     out_grad_hbm,
     h2,
-    out_w1s,
-    out_w1n,
-    out_w2s,
-    out_w2n,
+    w2_sum,
+    w1_sum_0,
+    w1_sum_1,
     features,
     serve_rows,
     row_counts,
+    index_rows,
     index_one,
     index_two,
     w2,
@@ -83,7 +86,12 @@
     self_t,
     count_t,
     back_out,
-    back_in,
+    back_in_0,
+    back_in_1,
+    back_mid_0,
+    back_mid_1,
+    back_end_0,
+    back_end_1,
     slope_own,
     slope_all,
     w2_total,
@@ -97,9 +105,12 @@
     my_store, my_feat = lax.axis_index("store"), lax.axis_index("feat")
     my_chip, my_core = my_store // 2, lax.rem(my_store, 2)
     n_chip = n_store // 2
+    n_x = 1 << (n_feat.bit_length() // 2)
+    n_y = n_feat // n_x
+    my_y, my_x = my_feat // n_x, lax.rem(my_feat, n_x)
     width, papers = features.shape
     cap = serve_rows.shape[2]
-    entries, nodes = index_one.shape[1:]
+    entries, nodes = index_one.shape
     fan_one = entries - 1
     fan_two = index_two.shape[1] - 1
     units, hidden = w2.shape[0] // 2, w2.shape[1]
@@ -107,6 +118,7 @@
     own_rows = nodes // n_feat
     pad = both.shape[0] // 2
     pending = []
+    back_in, back_mid, back_end = (back_in_0, back_in_1), (back_mid_0, back_mid_1), (back_end_0, back_end_1)
 
     def store_peer(step):
         return lax.rem(my_store + step + n_store, n_store)
@@ -147,6 +159,64 @@
         loop(1, n_feat, lambda k: send(src_of(feat_peer(k)), dst, name, recv_of(name), "feat", feat_peer(k)))
         keep(src_of(my_feat), dst, recv_of(name))
 
+    def along(x, k):
+        return my_y * n_x + lax.rem(my_x + k, n_x) if x else lax.rem(my_y + k, n_y) * n_x + my_x
+
+    def count_of(x):
+        return n_x if x else n_y
+
+    def spread_near(name, own, dst, x):
+        step, spot = name + "_near", dst.at[my_y, my_x]
+        loop(1, count_of(x), lambda k: send(own, spot, step, recv_of(step), "feat", along(x, k)))
+        keep(own, spot, recv_of(step))
+        if count_of(x) > 1:
+            later(dst.at[0, pl.ds(0, n_x - 1)] if x else dst.at[pl.ds(0, n_y - 1), 0], step)
+
+    def spread_far(name, dst, x):
+        step, line = name + "_far", dst.at[my_y] if x else dst.at[:, my_x]
+        await_bytes(line, recv_of(name + "_near"))
+        loop(1, count_of(not x), lambda k: send(line, line, step, recv_of(step), "feat", along(not x, k)))
+        if count_of(not x) > 1:
+            later(dst.at[pl.ds(0, n_y - 1)] if x else dst.at[:, pl.ds(0, n_x - 1)], step)
+
+    def spread_end(name, dst, x):
+        if count_of(not x) > 1:
+            await_bytes(dst.at[pl.ds(0, n_y - 1)] if x else dst.at[:, pl.ds(0, n_x - 1)], recv_of(name + "_far"))
+
+    def fold_far(name, src, dst, x):
+        step, mine = name + "_far", my_x if x else my_y
+
+        def lines(k):
+            return src.at[:, lax.rem(my_x + k, n_x)] if x else src.at[lax.rem(my_y + k, n_y)]
+
+        loop(1, count_of(x), lambda k: send(lines(k), dst.at[mine], step, recv_of(step), "feat", along(x, k)))
+        keep(lines(0), dst.at[mine], recv_of(step))
+        if count_of(x) > 1:
+            later(dst.at[pl.ds(0, count_of(x) - 1)], step)
+
+    def fold_near(name, src, middle, dst, x):
+        await_bytes(src, recv_of(name + "_far"))
+        total = src[0].astype(F32)
+        for line in range(1, count_of(x)):
+            total += src[line].astype(F32)
+        middle[...] = total.astype(BF16)
+        step, mine = name + "_near", my_y if x else my_x
+
+        def block(k):
+            return middle.at[lax.rem(my_y + k, n_y) if x else lax.rem(my_x + k, n_x)]
+
+        loop(1, count_of(not x), lambda k: send(block(k), dst.at[mine], step, recv_of(step), "feat", along(not x, k)))
+        keep(block(0), dst.at[mine], recv_of(step))
+        if count_of(not x) > 1:
+            later(dst.at[pl.ds(0, count_of(not x) - 1)], step)
+
+    def fold_end(name, src, x):
+        await_bytes(src, recv_of(name + "_near"))
+        total = src[0].astype(F32)
+        for line in range(1, count_of(not x)):
+            total += src[line].astype(F32)
+        return total
+
     barrier = pltpu.get_barrier_semaphore()
 
     def greet(axis, peer):
@@ -158,7 +228,7 @@
         (w1_self_hbm, w1_own.at[0]),
         (w1_neigh_hbm, w1_own.at[1]),
         (row_counts_hbm, row_counts),
-        (index_one_hbm, index_one),
+        (index_one_hbm, index_rows),
         (index_two_hbm, index_two),
         (w2_self_hbm, w2.at[pl.ds(0, units)]),
         (w2_neigh_hbm, w2.at[pl.ds(units, units)]),
@@ -186,9 +256,9 @@
         low, high_of = wanted & (LOW - 1), wanted // LOW
         one_hot = jnp.where(low_ids == low, 1.0, 0.0).astype(BF16)
         found = dot(table[...], one_hot)
-        total = jnp.zeros((width, cap), F32)
-        for high in range(highs):
-            total += jnp.where(high_of == high, found[high * width : (high + 1) * width, :], 0.0)
+        total = found[0:width, :]
+        for high in range(1, highs):
+            total = jnp.where(high_of == high, found[high * width : (high + 1) * width, :], total)
         stage[trainer] = total.astype(BF16)
 
     loop(0, n_store, serve)
@@ -223,7 +293,9 @@
     later(stage.at[pl.ds(0, n_store - 1)], "rows")
     later(w1_all.at[pl.ds(0, n_feat - 1), 0, pl.ds(0, width)], "w1")
 
-    raw = index_one[0]
+    for entry in range(entries):
+        index_one[entry : entry + 1, :] = index_rows[entry]
+    raw = index_one[...]
     owners = raw // cap
     place = (raw & (cap - 1)).astype(F32)
     counts = jnp.ones(raw.shape, F32)
@@ -250,25 +322,30 @@
 
     loop(0, nodes // strip, second_tables)
 
-    def gather(entry, group, at):
-        found = dot(rows_in[pl.ds(group * group_size, group_size)].reshape(group_size * width, cap), pick[entry])
-        of = owner_of[pl.ds(entry, 1), :]
-        total = both[at : at + width, :]
+    def gather(group):
+        await_bytes(rows_in.at[pl.ds(group * group_size, group_size)], group_sems.at[group])
+        arrived = rows_in[pl.ds(group * group_size, group_size)].reshape(group_size * width, cap)
+        owners = []
         for member in range(group_size):
             rank = group * group_size + member
-            offset = half_store - (rank + 1) // 2 if rank % 2 else rank // 2 - half_store
-            total += jnp.where(of == store_peer(-offset), found[member * width : (member + 1) * width, :], 0.0)
-        both[at : at + width, :] = total
-
-    for group in range(GROUPS):
-        await_bytes(rows_in.at[pl.ds(group * group_size, group_size)], group_sems.at[group])
-        gather(0, group, 0)
-        loop(1, entries, lambda entry, group=group: gather(entry, group, pad))
-        if group == GROUPS - 3:
-            await_bytes(w1_all.at[:, 0, pl.ds(0, width)], recv_of("w1"))
-            mine = w1_all.at[:, my_core, pl.ds(0, width)]
-            send(mine, mine, "w1_swap", recv_of("w1_swap"), "store", my_store + 1 - 2 * my_core)
-            later(w1_all.at[:, 0, pl.ds(0, width)], "w1_swap")
+            offset = half_store - (rank + 1) // 2 if member % 2 else rank // 2 - half_store
+            owners.append(store_peer(-offset))
+        sums = [both[0:width, :], both[pad : pad + width, :]]
+        for entry in range(entries):
+            found = dot(arrived, pick[entry])
+            of = owner_of[entry : entry + 1, :]
+            mine = jnp.zeros((width, nodes), F32)
+            for member in range(group_size):
+                mine = jnp.where(of == owners[member], found[member * width : (member + 1) * width, :], mine)
+            sums[min(entry, 1)] += mine
+        both[0:width, :], both[pad : pad + width, :] = sums
+
+    loop(0, GROUPS - 2, gather)
+    await_bytes(w1_all.at[:, 0, pl.ds(0, width)], recv_of("w1"))
+    mine = w1_all.at[:, my_core, pl.ds(0, width)]
+    send(mine, mine, "w1_swap", recv_of("w1_swap"), "store", my_store + 1 - 2 * my_core)
+    later(w1_all.at[:, 0, pl.ds(0, width)], "w1_swap")
+    loop(GROUPS - 2, GROUPS, gather)
     both[pad : pad + width, :] = both[pad : pad + width, :] / fan_one
     node_inputs = both[...].astype(BF16)
     turned = both[...].T.astype(BF16)
@@ -286,15 +363,15 @@
         cols = slice(half * columns, (half + 1) * columns)
         pre_one = dot(own_nodes, w1_all[:, :, :, cols].reshape(n_feat * 2 * pad, columns))
         hid_own[half] = (pre_one * jax.nn.sigmoid(pre_one)).astype(BF16)
-        name = f"hid{half}"
-        share(lambda peer, half=half: hid_own.at[half], hid_all.at[half, my_feat], name)
-        later(hid_all.at[half, pl.ds(0, n_feat - 1)], name)
+        spread_near(f"hid{half}", hid_own.at[half], hid_all.at[half], half == 0)
         slope_one.append(slope(pre_one))
+    for half in range(HALVES):
+        spread_far(f"hid{half}", hid_all.at[half], half == 0)
 
     mixed = jnp.zeros((2 * units, nodes), F32)
     hid = []
     for half in range(HALVES):
-        await_bytes(hid_all.at[half], recv_of(f"hid{half}"))
+        spread_end(f"hid{half}", hid_all.at[half], half == 0)
         hid.append(hid_all[half].reshape(nodes, columns))
         mixed += nt_dot(w2[:, half * columns : (half + 1) * columns], hid[half])
     upper, lower = halves(mixed)
@@ -308,15 +385,13 @@
     for half in range(HALVES):
         weights = w2[:, half * columns : (half + 1) * columns]
         back = dot(turned, jnp.concatenate([weights, weights], axis=0))
-        back_out[half] = back.astype(BF16).reshape(n_feat, own_rows, columns)
-        name = f"back{half}"
-        share(lambda peer, half=half: back_out.at[half, peer], back_in.at[half, my_feat], name)
-        later(back_out.at[half, pl.ds(0, n_feat - 1)], name)
+        back_out[half] = back.astype(BF16).reshape(n_y, n_x, own_rows, columns)
+        fold_far(f"back{half}", back_out.at[half], back_in[half], half == 1)
     h2[...] = (pre_two * jax.nn.sigmoid(pre_two)).astype(BF16)
 
     sibling = my_store + 1 - 2 * my_core
 
-    def total_of(ref, name):
+    def total_of(ref, total, name):
         tiles = ref.shape[1] // 2
         per = -(-tiles // n_chip)
         summers = tiles // per
@@ -328,8 +403,7 @@
         def first(chip):
             return (chip - chip // 4 if spread else chip) * per
 
-        part, merged = ref.at[0], ref.at[1]
-        arrived, total = ref.at[2], ref.at[3]
+        part, merged, arrived = ref.at[0], ref.at[1], ref.at[2]
 
         def fill(half, grad, row0=0):
             across = grad.shape[1] // 128
@@ -424,19 +498,12 @@
             send(mine, mine, name + "_swap", recv_of(name + "_swap"), "store", sibling)
             later(total.at[pl.ds(0, tiles)], name + "_swap")
 
-        def write(outs, col0, cols, rows):
+        def finish():
             await_bytes(total.at[pl.ds(0, tiles)], recv_of(name + "_swap"))
-            across = cols // 128
-            for half, out in enumerate(outs):
-                for row in range(rows // 16):
-                    for col in range(across):
-                        out[row * 16 : (row + 1) * 16, col0 + col * 128 : col0 + (col + 1) * 128] = total[
-                            half * tiles + row * across + col
-                        ].astype(F32)
-
-        return fill, merge, reduce, spread_out, swap, write
-
-    fill, merge, reduce2, spread2, swap2, write2 = total_of(w2_total, "w2")
+
+        return fill, merge, reduce, spread_out, swap, finish
+
+    fill, merge, reduce2, spread2, swap2, finish2 = total_of(w2_total, w2_sum, "w2")
     upper, lower = halves(node_grad)
     stacked = jnp.concatenate([upper, lower], axis=0)
     grad_w2 = jnp.concatenate([dot(stacked, part) for part in hid], axis=1)
@@ -447,22 +514,20 @@
     reduce2()
 
     for half in range(HALVES):
-        name = f"back{half}"
-        await_bytes(back_in.at[half], recv_of(name))
-        total = back_in[half, 0].astype(F32)
-        for group in range(1, n_feat):
-            total += back_in[half, group].astype(F32)
+        fold_near(f"back{half}", back_in[half], back_mid[half], back_end[half], half == 1)
+    for half in range(HALVES):
+        total = fold_end(f"back{half}", back_end[half], half == 1)
         slope_own[half] = (total * slope_one[half]).astype(BF16)
-        name = f"slope{half}"
-        share(lambda peer, half=half: slope_own.at[half], slope_all.at[half, my_feat], name)
-        later(slope_all.at[half, pl.ds(0, n_feat - 1)], name)
+        spread_near(f"slope{half}", slope_own.at[half], slope_all.at[half], half == 0)
+    for half in range(HALVES):
+        spread_far(f"slope{half}", slope_all.at[half], half == 0)
     spread2()
 
     steps = []
-    for half, ref in enumerate((w1_total_0, w1_total_1)):
-        await_bytes(slope_all.at[half], recv_of(f"slope{half}"))
+    for half, (ref, total) in enumerate(((w1_total_0, w1_sum_0), (w1_total_1, w1_sum_1))):
+        spread_end(f"slope{half}", slope_all.at[half], half == 0)
         grad_w1 = dot(node_inputs, slope_all[half].reshape(nodes, columns)).astype(BF16)
-        fill, merge, *rest = total_of(ref, f"w1_{half}")
+        fill, merge, *rest = total_of(ref, total, f"w1_{half}")
         steps.append(rest)
         fill(0, grad_w1[0:width])
         fill(1, grad_w1[pad : pad + width])
@@ -471,39 +536,73 @@
     swap2()
     steps[0][1]()
     steps[1][1]()
-    write2((out_w2s, out_w2n), 0, hidden, units)
     steps[0][2]()
     steps[1][2]()
-    steps[0][3]((out_w1s, out_w1n), 0, columns, width)
-    steps[1][3]((out_w1s, out_w1n), columns, columns, width)
+    finish2()
+    steps[0][3]()
+    steps[1][3]()
 
     for wait in pending:
         wait()
 
 
+def write_out(*refs):
+    from_hbm, outs, held, wide, sems = refs[:4], refs[4:9], refs[9:12], refs[12:16], refs[16]
+    to_out = [pltpu.make_async_copy(from_hbm[0], outs[0], sems.at[0])]
+    to_out[0].start()
+    reads = [pltpu.make_async_copy(src, dst, sems.at[1 + i]) for i, (src, dst) in enumerate(zip(from_hbm[1:], held))]
+    for read in reads:
+        read.start()
+    across = wide[2].shape[1] // 128
+    for part, where in enumerate((2, 3, 0, 1)):
+        if part == 0:
+            reads[0].wait()
+        if part == 2:
+            reads[1].wait()
+            reads[2].wait()
+        rows = wide[where].shape[0] // 16
+        for row in range(rows):
+            for col in range(across):
+                if part < 2:
+                    tile = held[0][(part * rows + row) * across + col]
+                else:
+                    each = across // HALVES
+                    tile = held[1 + col // each][((part - 2) * rows + row) * each + col % each]
+                wide[where][row * 16 : (row + 1) * 16, col * 128 : (col + 1) * 128] = tile.astype(F32)
+        to_out.append(pltpu.make_async_copy(wide[where], outs[where + 1], sems.at[4 + where]))
+        to_out[-1].start()
+    for copy in to_out:
+        copy.wait()
+
+
 def body(n_store, n_feat, *args):
+    args = list(args)
+    args[3] = jnp.transpose(args[3], (1, 0, 2))
     features, serve_rows, _, index_one, index_two, w1_self, _, w2_self, _, out_grad = args
     width, papers = features.shape
     cap = serve_rows.shape[2]
-    entries, nodes = index_one.shape[1:]
+    entries, _, nodes = index_one.shape
     targets = index_two.shape[2]
     hidden, units = w2_self.shape[1], w2_self.shape[0]
     own_rows = nodes // n_feat
     pad = -(-width // 64) * 64
     columns = hidden // HALVES
-    blocks = (HALVES, n_feat, own_rows, columns)
+    n_x = 1 << (n_feat.bit_length() // 2)
+    n_y = n_feat // n_x
+    blocks = (HALVES, n_y, n_x, own_rows, columns)
     tiles2 = units // 16 * (hidden // 128)
     tiles1 = width // 16 * (columns // 128)
 
     def total_scratch(tiles):
         per = -(-tiles // (n_store // 2))
-        return pltpu.VMEM((4, max(2 * tiles, n_store // 2 * per), 16, 128), BF16)
+        return pltpu.VMEM((3, max(2 * tiles, n_store // 2 * per), 16, 128), BF16)
 
     scratch = [
         pltpu.VMEM(features.shape, F32),
         pltpu.VMEM(serve_rows.shape, jnp.int32),
         pltpu.VMEM(args[2].shape, jnp.int32),
-        pltpu.VMEM(index_one.shape, jnp.int32),
+        pltpu.VMEM((entries, 1, nodes), jnp.int32),
+        pltpu.VMEM((entries, nodes), jnp.int32),
         pltpu.VMEM(index_two.shape, jnp.int32),
         pltpu.VMEM((2 * units, hidden), BF16),
         pltpu.VMEM(out_grad.shape, BF16),
@@ -522,7 +621,12 @@
         pltpu.VMEM((nodes, targets), BF16),
         pltpu.VMEM((nodes, targets), BF16),
         pltpu.VMEM(blocks, BF16),
-        pltpu.VMEM(blocks, BF16),
+        pltpu.VMEM((n_y, n_x, own_rows, columns), BF16),
+        pltpu.VMEM((n_x, n_y, own_rows, columns), BF16),
+        pltpu.VMEM((n_x, own_rows, columns), BF16),
+        pltpu.VMEM((n_y, own_rows, columns), BF16),
+        pltpu.VMEM((n_x, own_rows, columns), BF16),
+        pltpu.VMEM((n_y, own_rows, columns), BF16),
         pltpu.VMEM((HALVES, own_rows, columns), BF16),
         pltpu.VMEM(blocks, BF16),
         total_scratch(tiles2),
@@ -533,22 +637,38 @@
         pltpu.SemaphoreType.DMA((len(SENDS),)),
         pltpu.SemaphoreType.DMA((GROUPS,)),
     ]
-    return pl.pallas_call(
+    h2, *sums = pl.pallas_call(
         functools.partial(kernel, n_store, n_feat),
         out_shape=[
             jax.ShapeDtypeStruct((units, targets), BF16),
-            jax.ShapeDtypeStruct((width, hidden), F32),
-            jax.ShapeDtypeStruct((width, hidden), F32),
-            jax.ShapeDtypeStruct((units, hidden), F32),
-            jax.ShapeDtypeStruct((units, hidden), F32),
+            jax.ShapeDtypeStruct((2 * tiles2, 16, 128), BF16),
+            jax.ShapeDtypeStruct((2 * tiles1, 16, 128), BF16),
+            jax.ShapeDtypeStruct((2 * tiles1, 16, 128), BF16),
         ],
-        in_specs=[pl.BlockSpec(memory_space=pl.ANY)] * len(args),
-        out_specs=[pl.BlockSpec(memory_space=pltpu.VMEM)] * 5,
+        in_specs=[pl.BlockSpec(memory_space=pltpu.HBM)] * len(args),
+        out_specs=[pl.BlockSpec(memory_space=pltpu.VMEM)] * 4,
         scratch_shapes=scratch,
         compiler_params=pltpu.CompilerParams(
-            collective_id=0, has_side_effects=True, vmem_limit_bytes=48 * 1024 * 1024
+            collective_id=0, has_side_effects=True, vmem_limit_bytes=VMEM_LIMIT
         ),
     )(*args)
+    outs = [
+        jax.ShapeDtypeStruct((units, targets), BF16),
+        jax.ShapeDtypeStruct((width, hidden), F32),
+        jax.ShapeDtypeStruct((width, hidden), F32),
+        jax.ShapeDtypeStruct((units, hidden), F32),
+        jax.ShapeDtypeStruct((units, hidden), F32),
+    ]
+    return pl.pallas_call(
+        write_out,
+        out_shape=outs,
+        in_specs=[pl.BlockSpec(memory_space=pltpu.HBM)] * 4,
+        out_specs=[pl.BlockSpec(memory_space=pltpu.HBM)] * 5,
+        scratch_shapes=[pltpu.VMEM(total.shape, BF16) for total in sums]
+        + [pltpu.VMEM(out.shape, F32) for out in outs[1:]]
+        + [pltpu.SemaphoreType.DMA((8,))],
+        compiler_params=pltpu.CompilerParams(vmem_limit_bytes=VMEM_LIMIT),
+    )(h2, *sums)
 
 
 def solution(mesh):

time: 139 us -> 125 us (0.90)
  local copies, waits for them, and re-layouts: 10.5 us -> 0 us
  Pallas kernels: 127 us -> 125 us
    unnamed x24 -> x0, local copies, waits for them, and re-layouts: 10.5 us -> none
    pallas_call x1, Pallas kernels: 127 us -> 121 us  [body(): pl.pallas_call(functools.partial(kernel, n_store, n_feat), out_shape=[jax...]
    pallas_call x0 -> x1, Pallas kernels: none -> 3.17 us  [body(): pl.pallas_call(write_out, out_shape=outs, in_specs=[pl.BlockSpec(memory_s...]
where the time goes in v3:
time: 125 us
  Pallas kernels  125 us (100%)
    pallas_call x1, Pallas kernels, body(): pl.pallas_call(functools.partial(kernel, n_store, n_feat), out_shape=[jax...  121 us
    pallas_call x1, Pallas kernels, body(): pl.pallas_call(write_out, out_shape=outs, in_specs=[pl.BlockSpec(memory_s...  3.17 us

profile of v3, /device:TPU:1, one launch (start us, length us, event | category | flops | bytes accessed | tf_op | source)
XLA Modules:
  0.0 125.2 jit_solution(8703116636646032895)
XLA Ops:
  0.6 121.4 %shard_map.137 = (bf16[64,512]{1,0:T(8,128)(2,1)}, bf16[64,16,128]{2,1,0:T(8,128)(2,1)}, bf16[24,16,128]{2,1,0:T(8,128)(2,1)}, bf16[24,16,128]{2,1,0:T(8,128)(2,1)}) custom-call(f32[48,4096]{1,0:T(8,128)} %features_hbm.1, s32[1,32,256]{2,1,0:T(8,128)} %serve_rows_hbm.1, s32[1,32]{1,0:T(1,128)} %row_counts_hbm.1, s32[11,1,512]{2,1,0:T(1,128)} %bitcast.1, ...), custom_call_target="tpu_custom_call" | custom-call | tf_op jit(solution)/shard_map/pallas_call | solution.py:640
  122.0 3.2 %shard_map.138 = (bf16[64,512]{1,0:T(8,128)(2,1)}, f32[48,1024]{1,0:T(8,128)}, f32[48,1024]{1,0:T(8,128)}, f32[64,1024]{1,0:T(8,128)}, f32[64,1024]{1,0:T(8,128)}) custom-call(bf16[64,512]{1,0:T(8,128)(2,1)} %get-tuple-element.9.refs_0_, bf16[64,16,128]{2,1,0:T(8,128)(2,1)} %get-tuple-element.10.refs_1_, bf16[24,16,128]{2,1,0:T(8,128)(2,1)} %get-tuple-element.11.refs_2_, ...), custom_call_target="tpu_custom_call" | custom-call | tf_op jit(solution)/shard_map/pallas_call | solution.py:662

commit v4 on v3

--- a/solution.py
+++ b/solution.py
@@ -37,12 +37,14 @@
 
 SENDS = (
     ("rows", "w1", "w1_swap", "nodes")
-    + tuple(what + half + step for what in ("hid", "back", "slope") for half in "01" for step in ("_near", "_far"))
+    + ("inputs", "sibling0", "sibling1")
+    + tuple(what + quarter + step for what in ("hid", "back", "slope") for quarter in "0123" for step in ("_near", "_far"))
     + tuple(total + step for total in ("w2", "w1_0", "w1_1") for step in ("_merge", "_reduce", "_spread", "_swap"))
 )
 INPUTS = 10
 GROUPS = 8
-HALVES = 2
+QUARTERS = 4
+STAGES = ((0, 2), (1, 3))
 VMEM_LIMIT = 60 * 1024 * 1024
 
 
@@ -77,6 +79,7 @@
     owner_of,
     pick,
     both,
+    node_inputs,
     nodes_out,
     nodes_in,
     w1_own,
@@ -114,11 +117,14 @@
     fan_one = entries - 1
     fan_two = index_two.shape[1] - 1
     units, hidden = w2.shape[0] // 2, w2.shape[1]
-    columns = hidden // HALVES
+    columns = hidden // QUARTERS
     own_rows = nodes // n_feat
     pad = both.shape[0] // 2
     pending = []
-    back_in, back_mid, back_end = (back_in_0, back_in_1), (back_mid_0, back_mid_1), (back_end_0, back_end_1)
+    back_in = (back_in_0.at[0], back_in_0.at[1], back_in_1.at[0], back_in_1.at[1])
+    back_mid = (back_mid_0.at[0], back_mid_0.at[1], back_mid_1.at[0], back_mid_1.at[1])
+    back_end = (back_end_0.at[0], back_end_0.at[1], back_end_1.at[0], back_end_1.at[1])
+    sibling = my_store + 1 - 2 * my_core
 
     def store_peer(step):
         return lax.rem(my_store + step + n_store, n_store)
@@ -347,7 +353,9 @@
     later(w1_all.at[:, 0, pl.ds(0, width)], "w1_swap")
     loop(GROUPS - 2, GROUPS, gather)
     both[pad : pad + width, :] = both[pad : pad + width, :] / fan_one
-    node_inputs = both[...].astype(BF16)
+    node_inputs[my_core] = both[...].astype(BF16)
+    send(node_inputs.at[my_core], node_inputs.at[my_core], "inputs", recv_of("inputs"), "store", sibling)
+    later(node_inputs.at[0], "inputs")
     turned = both[...].T.astype(BF16)
     for group in range(n_feat):
         nodes_out[group] = turned[group * own_rows : (group + 1) * own_rows, :]
@@ -358,22 +366,25 @@
     await_bytes(w1_all.at[:, 0, pl.ds(0, width)], recv_of("w1_swap"))
     await_bytes(nodes_in, recv_of("nodes"))
     own_nodes = jnp.concatenate([nodes_in[group] for group in range(n_feat)], axis=1)
-    slope_one = []
-    for half in range(HALVES):
-        cols = slice(half * columns, (half + 1) * columns)
-        pre_one = dot(own_nodes, w1_all[:, :, :, cols].reshape(n_feat * 2 * pad, columns))
-        hid_own[half] = (pre_one * jax.nn.sigmoid(pre_one)).astype(BF16)
-        spread_near(f"hid{half}", hid_own.at[half], hid_all.at[half], half == 0)
-        slope_one.append(slope(pre_one))
-    for half in range(HALVES):
-        spread_far(f"hid{half}", hid_all.at[half], half == 0)
+    slope_one = [None] * QUARTERS
+    for stage_now in STAGES:
+        for q in stage_now:
+            cols = slice(q * columns, (q + 1) * columns)
+            pre_one = dot(own_nodes, w1_all[:, :, :, cols].reshape(n_feat * 2 * pad, columns))
+            hid_own[q] = (pre_one * jax.nn.sigmoid(pre_one)).astype(BF16)
+            spread_near(f"hid{q}", hid_own.at[q], hid_all.at[q], q < 2)
+            slope_one[q] = slope(pre_one)
+    for stage_now in STAGES:
+        for q in stage_now:
+            spread_far(f"hid{q}", hid_all.at[q], q < 2)
 
     mixed = jnp.zeros((2 * units, nodes), F32)
-    hid = []
-    for half in range(HALVES):
-        spread_end(f"hid{half}", hid_all.at[half], half == 0)
-        hid.append(hid_all[half].reshape(nodes, columns))
-        mixed += nt_dot(w2[:, half * columns : (half + 1) * columns], hid[half])
+    hid = [None] * QUARTERS
+    for stage_now in STAGES:
+        for q in stage_now:
+            spread_end(f"hid{q}", hid_all.at[q], q < 2)
+            hid[q] = hid_all[q].reshape(nodes, columns)
+            mixed += nt_dot(w2[:, q * columns : (q + 1) * columns], hid[q])
     upper, lower = halves(mixed)
     self_term = dot(jnp.concatenate([upper[:units], lower[:units]], axis=0), self_t[...])
     neigh_term = dot(jnp.concatenate([upper[units:], lower[units:]], axis=0), count_t[...])
@@ -382,16 +393,15 @@
     node_grad = jnp.concatenate([nt_dot(grad_two, self_t[...]), nt_dot(grad_two, count_t[...]) / fan_two], axis=0)
     upper, lower = halves(node_grad.T)
     turned = jnp.concatenate([upper, lower], axis=1)
-    for half in range(HALVES):
-        weights = w2[:, half * columns : (half + 1) * columns]
-        back = dot(turned, jnp.concatenate([weights, weights], axis=0))
-        back_out[half] = back.astype(BF16).reshape(n_y, n_x, own_rows, columns)
-        fold_far(f"back{half}", back_out.at[half], back_in[half], half == 1)
+    for stage_now in STAGES:
+        for q in stage_now:
+            weights = w2[:, q * columns : (q + 1) * columns]
+            back = dot(turned, jnp.concatenate([weights, weights], axis=0))
+            back_out[q] = back.astype(BF16).reshape(n_y, n_x, own_rows, columns)
+            fold_far(f"back{q}", back_out.at[q], back_in[q], q >= 2)
     h2[...] = (pre_two * jax.nn.sigmoid(pre_two)).astype(BF16)
 
-    sibling = my_store + 1 - 2 * my_core
-
-    def total_of(ref, total, name):
+    def total_of(ref, total, name, merged_already=False):
         tiles = ref.shape[1] // 2
         per = -(-tiles // n_chip)
         summers = tiles // per
@@ -409,9 +419,11 @@
             across = grad.shape[1] // 128
             for row in range(grad.shape[0] // 16):
                 for col in range(across):
-                    part[half * tiles + row * across + col] = grad[
-                        row * 16 : (row + 1) * 16, col * 128 : (col + 1) * 128
-                    ]
+                    tile = grad[row * 16 : (row + 1) * 16, col * 128 : (col + 1) * 128]
+                    if merged_already:
+                        merged[tiles + row * across + col] = tile
+                    else:
+                        part[half * tiles + row * across + col] = tile
 
         def merge():
             own = pl.ds((1 - my_core) * tiles, tiles)
@@ -419,9 +431,10 @@
             later(part.at[pl.ds(0, tiles)], name + "_merge")
 
         def reduce():
-            await_bytes(merged.at[pl.ds(0, tiles)], recv_of(name + "_merge"))
-            both_cores = part[pl.ds(my_core * tiles, tiles)].astype(F32) + merged[0:tiles].astype(F32)
-            merged[tiles : 2 * tiles] = both_cores.astype(BF16)
+            if not merged_already:
+                await_bytes(merged.at[pl.ds(0, tiles)], recv_of(name + "_merge"))
+                both_cores = part[pl.ds(my_core * tiles, tiles)].astype(F32) + merged[0:tiles].astype(F32)
+                merged[tiles : 2 * tiles] = both_cores.astype(BF16)
 
             def to(k):
                 chip = chip_peer(k)
@@ -513,34 +526,105 @@
     merge()
     reduce2()
 
-    for half in range(HALVES):
-        fold_near(f"back{half}", back_in[half], back_mid[half], back_end[half], half == 1)
-    for half in range(HALVES):
-        total = fold_end(f"back{half}", back_end[half], half == 1)
-        slope_own[half] = (total * slope_one[half]).astype(BF16)
-        spread_near(f"slope{half}", slope_own.at[half], slope_all.at[half], half == 0)
-    for half in range(HALVES):
-        spread_far(f"slope{half}", slope_all.at[half], half == 0)
+    def slope_near(stage_no):
+        for core, q in enumerate(STAGES[stage_no]):
+            x, step, spot = core == 0, f"slope{q}_near", slope_all.at[stage_no, my_core, my_y, my_x]
+            arrival = recv_of(f"slope{stage_no}_near")
+            total = fold_end(f"back{q}", back_end[q], q >= 2)
+            slope_own[q] = (total * slope_one[q]).astype(BF16)
+
+            def to_line(k, x=x, step=step, spot=spot, arrival=arrival, core=core, q=q):
+                chip = along(x, k)
+                pltpu.make_async_remote_copy(
+                    src_ref=slope_own.at[q],
+                    dst_ref=spot,
+                    send_sem=send_sems.at[SENDS.index(step)],
+                    recv_sem=arrival,
+                    device_id={"store": my_chip * 2 + core, "feat": chip},
+                    device_id_type=MESH,
+                ).start()
+
+            loop(1, count_of(x), to_line)
+            if count_of(x) > 1:
+                later(slope_all.at[0, 0, 0, pl.ds(0, n_x - 1)] if x else slope_all.at[0, 0, pl.ds(0, n_y - 1), 0], step)
+
+            if core == 0:
+                later(slope_own.at[0], f"sibling{stage_no}")
+
+            @pl.when(my_core == core)
+            def _(arrival=arrival, q=q, spot=spot):
+                keep(slope_own.at[q], spot, arrival)
+
+            @pl.when(my_core != core)
+            def _(arrival=arrival, q=q, spot=spot):
+                send(slope_own.at[q], spot, f"sibling{stage_no}", arrival, "store", sibling)
+
+    def slope_line(stage_no, x):
+        return slope_all.at[stage_no, :, my_y] if x else slope_all.at[stage_no, :, :, my_x]
+
+    def slope_rest(stage_no, x):
+        return slope_all.at[stage_no, :, pl.ds(0, n_y - 1)] if x else slope_all.at[stage_no, :, :, pl.ds(0, n_x - 1)]
+
+    def on_core(core, fn):
+        pl.when(my_core == core)(fn)
+
+    def slope_far(stage_no):
+        step = f"slope{stage_no}_far"
+        for core in range(2):
+            x = core == 0
+
+            def forward(x=x):
+                line = slope_line(stage_no, x)
+                await_bytes(line, recv_of(f"slope{stage_no}_near"))
+                loop(1, count_of(not x), lambda k: send(line, line, step, recv_of(step), "feat", along(not x, k)))
+
+            on_core(core, forward)
+
+    def slope_end(stage_no, sems):
+        for core in range(2):
+            x = core == 0
+            if count_of(not x) > 1:
+                on_core(
+                    core,
+                    lambda x=x: await_bytes(slope_rest(stage_no, x), sems.at[SENDS.index(f"slope{stage_no}_far")]),
+                )
+
+    def first_weights(stage_no, fill):
+        slope_end(stage_no, recv_sems)
+        grad = jnp.zeros((2 * pad, columns), F32)
+        for core in range(2):
+            grad += dot(node_inputs[core], slope_all[stage_no, core].reshape(nodes, columns))
+        grad = grad.astype(BF16)
+        fill(0, jnp.concatenate([grad[0:width], grad[pad : pad + width]], axis=0))
+
+    def fold_middle(stage_no):
+        for q in STAGES[stage_no]:
+            fold_near(f"back{q}", back_in[q], back_mid[q], back_end[q], q >= 2)
+
+    fill_a, _, reduce_a, spread_a, swap_a, finish_a = total_of(w1_total_0, w1_sum_0, "w1_0", merged_already=True)
+    fill_b, _, reduce_b, spread_b, swap_b, finish_b = total_of(w1_total_1, w1_sum_1, "w1_1", merged_already=True)
+    fold_middle(0)
+    fold_middle(1)
+    slope_near(0)
+    slope_near(1)
+    slope_far(0)
+    slope_far(1)
     spread2()
-
-    steps = []
-    for half, (ref, total) in enumerate(((w1_total_0, w1_sum_0), (w1_total_1, w1_sum_1))):
-        spread_end(f"slope{half}", slope_all.at[half], half == 0)
-        grad_w1 = dot(node_inputs, slope_all[half].reshape(nodes, columns)).astype(BF16)
-        fill, merge, *rest = total_of(ref, total, f"w1_{half}")
-        steps.append(rest)
-        fill(0, grad_w1[0:width])
-        fill(1, grad_w1[pad : pad + width])
-        merge()
-        rest[0]()
+    await_bytes(node_inputs.at[0], recv_of("inputs"))
+    first_weights(0, fill_a)
+    reduce_a()
+    first_weights(1, fill_b)
+    reduce_b()
     swap2()
-    steps[0][1]()
-    steps[1][1]()
-    steps[0][2]()
-    steps[1][2]()
+    spread_a()
+    spread_b()
+    swap_a()
+    swap_b()
     finish2()
-    steps[0][3]()
-    steps[1][3]()
+    finish_a()
+    finish_b()
+    pending.append(lambda: slope_end(0, send_sems))
+    pending.append(lambda: slope_end(1, send_sems))
 
     for wait in pending:
         wait()
@@ -566,8 +650,10 @@
                 if part < 2:
                     tile = held[0][(part * rows + row) * across + col]
                 else:
-                    each = across // HALVES
-                    tile = held[1 + col // each][((part - 2) * rows + row) * each + col % each]
+                    each = across // QUARTERS
+                    quarter = col // each
+                    at = quarter // 2 * (2 * rows) + (part - 2) * rows + row
+                    tile = held[1 + quarter % 2][at * each + col % each]
                 wide[where][row * 16 : (row + 1) * 16, col * 128 : (col + 1) * 128] = tile.astype(F32)
         to_out.append(pltpu.make_async_copy(wide[where], outs[where + 1], sems.at[4 + where]))
         to_out[-1].start()
@@ -586,12 +672,12 @@
     hidden, units = w2_self.shape[1], w2_self.shape[0]
     own_rows = nodes // n_feat
     pad = -(-width // 64) * 64
-    columns = hidden // HALVES
+    columns = hidden // QUARTERS
     n_x = 1 << (n_feat.bit_length() // 2)
     n_y = n_feat // n_x
-    blocks = (HALVES, n_y, n_x, own_rows, columns)
+    blocks = (QUARTERS, n_y, n_x, own_rows, columns)
     tiles2 = units // 16 * (hidden // 128)
-    tiles1 = width // 16 * (columns // 128)
+    tiles1 = 2 * width // 16 * (columns // 128)
 
     def total_scratch(tiles):
         per = -(-tiles // (n_store // 2))
@@ -612,23 +698,24 @@
         pltpu.VMEM((entries, nodes), jnp.int32),
         pltpu.VMEM((entries, cap, nodes), BF16),
         pltpu.VMEM((2 * pad, nodes), F32),
+        pltpu.VMEM((2, 2 * pad, nodes), BF16),
         pltpu.VMEM((n_feat, own_rows, 2 * pad), BF16),
         pltpu.VMEM((n_feat, own_rows, 2 * pad), BF16),
         pltpu.VMEM((2, width, hidden), BF16),
         pltpu.VMEM((n_feat, 2, pad, hidden), BF16),
-        pltpu.VMEM((HALVES, own_rows, columns), BF16),
+        pltpu.VMEM((QUARTERS, own_rows, columns), BF16),
         pltpu.VMEM(blocks, BF16),
         pltpu.VMEM((nodes, targets), BF16),
         pltpu.VMEM((nodes, targets), BF16),
         pltpu.VMEM(blocks, BF16),
-        pltpu.VMEM((n_y, n_x, own_rows, columns), BF16),
-        pltpu.VMEM((n_x, n_y, own_rows, columns), BF16),
-        pltpu.VMEM((n_x, own_rows, columns), BF16),
-        pltpu.VMEM((n_y, own_rows, columns), BF16),
-        pltpu.VMEM((n_x, own_rows, columns), BF16),
-        pltpu.VMEM((n_y, own_rows, columns), BF16),
-        pltpu.VMEM((HALVES, own_rows, columns), BF16),
-        pltpu.VMEM(blocks, BF16),
+        pltpu.VMEM((2, n_y, n_x, own_rows, columns), BF16),
+        pltpu.VMEM((2, n_x, n_y, own_rows, columns), BF16),
+        pltpu.VMEM((2, n_x, own_rows, columns), BF16),
+        pltpu.VMEM((2, n_y, own_rows, columns), BF16),
+        pltpu.VMEM((2, n_x, own_rows, columns), BF16),
+        pltpu.VMEM((2, n_y, own_rows, columns), BF16),
+        pltpu.VMEM((QUARTERS, own_rows, columns), BF16),
+        pltpu.VMEM((2, 2, n_y, n_x, own_rows, columns), BF16),
         total_scratch(tiles2),
         total_scratch(tiles1),
         total_scratch(tiles1),

time: 125 us -> 121 us (0.968)
  Pallas kernels: 125 us -> 120 us
    pallas_call x1, Pallas kernels: 121 us -> 117 us  [body(): pl.pallas_call(functools.partial(kernel, n_store, n_feat), out_shape=[jax...]
where the time goes in v4:
time: 121 us
  Pallas kernels  120 us (99%)
    pallas_call x1, Pallas kernels, body(): pl.pallas_call(functools.partial(kernel, n_store, n_feat), out_shape=[jax...  117 us
    pallas_call x1, Pallas kernels, body(): pl.pallas_call(write_out, out_shape=outs, in_specs=[pl.BlockSpec(memory_s...  3.17 us

profile of v4, /device:TPU:1, one launch (start us, length us, event | category | flops | bytes accessed | tf_op | source)
XLA Modules:
  0.0 120.8 jit_solution(12023708051794631535)
XLA Ops:
  0.6 117.0 %shard_map.137 = (bf16[64,512]{1,0:T(8,128)(2,1)}, bf16[64,16,128]{2,1,0:T(8,128)(2,1)}, bf16[24,16,128]{2,1,0:T(8,128)(2,1)}, bf16[24,16,128]{2,1,0:T(8,128)(2,1)}) custom-call(f32[48,4096]{1,0:T(8,128)} %features_hbm.1, s32[1,32,256]{2,1,0:T(8,128)} %serve_rows_hbm.1, s32[1,32]{1,0:T(1,128)} %row_counts_hbm.1, s32[11,1,512]{2,1,0:T(1,128)} %bitcast.1, ...), custom_call_target="tpu_custom_call" | custom-call | tf_op jit(solution)/shard_map/pallas_call | solution.py:727
  117.7 3.2 %shard_map.138 = (bf16[64,512]{1,0:T(8,128)(2,1)}, f32[48,1024]{1,0:T(8,128)}, f32[48,1024]{1,0:T(8,128)}, f32[64,1024]{1,0:T(8,128)}, f32[64,1024]{1,0:T(8,128)}) custom-call(bf16[64,512]{1,0:T(8,128)(2,1)} %get-tuple-element.9.refs_0_, bf16[64,16,128]{2,1,0:T(8,128)(2,1)} %get-tuple-element.10.refs_1_, bf16[24,16,128]{2,1,0:T(8,128)(2,1)} %get-tuple-element.11.refs_2_, ...), custom_call_target="tpu_custom_call" | custom-call | tf_op jit(solution)/shard_map/pallas_call | solution.py:749

commit v5 on v4

--- a/solution.py
+++ b/solution.py
@@ -61,10 +61,11 @@
     w2_self_hbm,
     w2_neigh_hbm,
     out_grad_hbm,
-    h2,
-    w2_sum,
-    w1_sum_0,
-    w1_sum_1,
+    h2_hbm,
+    w1_self_out,
+    w1_neigh_out,
+    w2_self_out,
+    w2_neigh_out,
     features,
     serve_rows,
     row_counts,
@@ -100,7 +101,14 @@
     w2_total,
     w1_total_0,
     w1_total_1,
+    w2_sum,
+    w1_sum_0,
+    w1_sum_1,
+    h2,
+    w1_wide,
+    w2_wide,
     input_sems,
+    output_sems,
     send_sems,
     recv_sems,
     group_sems,
@@ -154,6 +162,11 @@
     def keep(src, dst, sem):
         pltpu.make_async_copy(src, dst, sem).start()
 
+    def write(src, dst, i):
+        copy = pltpu.make_async_copy(src, dst, output_sems.at[i])
+        copy.start()
+        pending.append(copy.wait)
+
     def loop(low, high, fn):
         def step(k, carry):
             fn(k)
@@ -241,10 +254,18 @@
         (out_grad_hbm, out_grad),
     )
     reads = [pltpu.make_async_copy(src, dst, input_sems.at[i]) for i, (src, dst) in enumerate(reads)]
-    for read in reads:
+    for read in reads[:2]:
         read.start()
-    loop(1, n_store, lambda k: greet("store", store_peer(k)))
+
+    def greet_pair(i):
+        greet("store", store_peer(n_store // 2 - i))
+        greet("store", store_peer(i - n_store // 2))
+
+    greet("store", store_peer(n_store // 2))
+    loop(1, n_store // 2, greet_pair)
     loop(1, n_feat, lambda k: greet("feat", feat_peer(k)))
+    for read in reads[2:]:
+        read.start()
     for group in range(n_feat):
         for half in range(2):
             w1_all[group, half, width:, :] = jnp.zeros((pad - width, hidden), BF16)
@@ -400,6 +421,7 @@
             back_out[q] = back.astype(BF16).reshape(n_y, n_x, own_rows, columns)
             fold_far(f"back{q}", back_out.at[q], back_in[q], q >= 2)
     h2[...] = (pre_two * jax.nn.sigmoid(pre_two)).astype(BF16)
+    write(h2, h2_hbm, 0)
 
     def total_of(ref, total, name, merged_already=False):
         tiles = ref.shape[1] // 2
@@ -618,11 +640,30 @@
     swap2()
     spread_a()
     spread_b()
+    finish2()
+    across = hidden // 128
+    for part, out in enumerate((w2_self_out, w2_neigh_out)):
+        for row in range(units // 16):
+            for col in range(across):
+                w2_wide[part, row * 16 : (row + 1) * 16, col * 128 : (col + 1) * 128] = w2_sum[
+                    (part * (units // 16) + row) * across + col
+                ].astype(F32)
+        write(w2_wide.at[part], out, 3 + part)
     swap_a()
     swap_b()
-    finish2()
-    finish_a()
-    finish_b()
+    each = across // QUARTERS
+    for stage_no, (finish, total) in enumerate(((finish_a, w1_sum_0), (finish_b, w1_sum_1))):
+        finish()
+        for core, q in enumerate(STAGES[stage_no]):
+            for row in range(2 * width // 16):
+                part, at = row // (width // 16), row % (width // 16) * 16
+                for col in range(each):
+                    left = (q * each + col) * 128
+                    w1_wide[part, at : at + 16, left : left + 128] = total[
+                        (core * (2 * width // 16) + row) * each + col
+                    ].astype(F32)
+    write(w1_wide.at[0], w1_self_out, 1)
+    write(w1_wide.at[1], w1_neigh_out, 2)
     pending.append(lambda: slope_end(0, send_sems))
     pending.append(lambda: slope_end(1, send_sems))
 
@@ -630,34 +671,11 @@
         wait()
 
 
-def write_out(*refs):
-    from_hbm, outs, held, wide, sems = refs[:4], refs[4:9], refs[9:12], refs[12:16], refs[16]
-    to_out = [pltpu.make_async_copy(from_hbm[0], outs[0], sems.at[0])]
-    to_out[0].start()
-    reads = [pltpu.make_async_copy(src, dst, sems.at[1 + i]) for i, (src, dst) in enumerate(zip(from_hbm[1:], held))]
-    for read in reads:
-        read.start()
-    across = wide[2].shape[1] // 128
-    for part, where in enumerate((2, 3, 0, 1)):
-        if part == 0:
-            reads[0].wait()
-        if part == 2:
-            reads[1].wait()
-            reads[2].wait()
-        rows = wide[where].shape[0] // 16
-        for row in range(rows):
-            for col in range(across):
-                if part < 2:
-                    tile = held[0][(part * rows + row) * across + col]
-                else:
-                    each = across // QUARTERS
-                    quarter = col // each
-                    at = quarter // 2 * (2 * rows) + (part - 2) * rows + row
-                    tile = held[1 + quarter % 2][at * each + col % each]
-                wide[where][row * 16 : (row + 1) * 16, col * 128 : (col + 1) * 128] = tile.astype(F32)
-        to_out.append(pltpu.make_async_copy(wide[where], outs[where + 1], sems.at[4 + where]))
-        to_out[-1].start()
-    for copy in to_out:
+def hand_over(*refs):
+    copies = [pltpu.make_async_copy(refs[i], refs[5 + i], refs[10].at[i]) for i in range(5)]
+    for copy in copies:
+        copy.start()
+    for copy in copies:
         copy.wait()
 
 
@@ -719,26 +737,18 @@
         total_scratch(tiles2),
         total_scratch(tiles1),
         total_scratch(tiles1),
+        pltpu.VMEM((2 * tiles2, 16, 128), BF16),
+        pltpu.VMEM((2 * tiles1, 16, 128), BF16),
+        pltpu.VMEM((2 * tiles1, 16, 128), BF16),
+        pltpu.VMEM((units, targets), BF16),
+        pltpu.VMEM((2, width, hidden), F32),
+        pltpu.VMEM((2, units, hidden), F32),
         pltpu.SemaphoreType.DMA((INPUTS,)),
+        pltpu.SemaphoreType.DMA((5,)),
         pltpu.SemaphoreType.DMA((len(SENDS),)),
         pltpu.SemaphoreType.DMA((len(SENDS),)),
         pltpu.SemaphoreType.DMA((GROUPS,)),
     ]
-    h2, *sums = pl.pallas_call(
-        functools.partial(kernel, n_store, n_feat),
-        out_shape=[
-            jax.ShapeDtypeStruct((units, targets), BF16),
-            jax.ShapeDtypeStruct((2 * tiles2, 16, 128), BF16),
-            jax.ShapeDtypeStruct((2 * tiles1, 16, 128), BF16),
-            jax.ShapeDtypeStruct((2 * tiles1, 16, 128), BF16),
-        ],
-        in_specs=[pl.BlockSpec(memory_space=pltpu.HBM)] * len(args),
-        out_specs=[pl.BlockSpec(memory_space=pltpu.VMEM)] * 4,
-        scratch_shapes=scratch,
-        compiler_params=pltpu.CompilerParams(
-            collective_id=0, has_side_effects=True, vmem_limit_bytes=VMEM_LIMIT
-        ),
-    )(*args)
     outs = [
         jax.ShapeDtypeStruct((units, targets), BF16),
         jax.ShapeDtypeStruct((width, hidden), F32),
@@ -746,16 +756,22 @@
         jax.ShapeDtypeStruct((units, hidden), F32),
         jax.ShapeDtypeStruct((units, hidden), F32),
     ]
+    found = pl.pallas_call(
+        functools.partial(kernel, n_store, n_feat),
+        out_shape=outs,
+        in_specs=[pl.BlockSpec(memory_space=pltpu.HBM)] * len(args),
+        out_specs=[pl.BlockSpec(memory_space=pltpu.HBM)] * 5,
+        scratch_shapes=scratch,
+        compiler_params=pltpu.CompilerParams(collective_id=0, has_side_effects=True, vmem_limit_bytes=VMEM_LIMIT),
+    )(*args)
     return pl.pallas_call(
-        write_out,
+        hand_over,
         out_shape=outs,
-        in_specs=[pl.BlockSpec(memory_space=pltpu.HBM)] * 4,
+        in_specs=[pl.BlockSpec(memory_space=pltpu.HBM)] * 5,
         out_specs=[pl.BlockSpec(memory_space=pltpu.HBM)] * 5,
-        scratch_shapes=[pltpu.VMEM(total.shape, BF16) for total in sums]
-        + [pltpu.VMEM(out.shape, F32) for out in outs[1:]]
-        + [pltpu.SemaphoreType.DMA((8,))],
+        scratch_shapes=[pltpu.SemaphoreType.DMA((5,))],
         compiler_params=pltpu.CompilerParams(vmem_limit_bytes=VMEM_LIMIT),
-    )(h2, *sums)
+    )(*found)
 
 
 def solution(mesh):

time: 121 us -> 149 us (1.23)
  Pallas kernels: 120 us -> 148 us
    pallas_call x2, Pallas kernels: 120 us -> 148 us  [the longest x1 117 us: body(): pl.pallas_call(functools.partial(kernel, n_store, n_feat), out_shape=outs...]
where the time goes in v5:
time: 149 us
  Pallas kernels  148 us (99%)
    pallas_call x1, Pallas kernels, body(): pl.pallas_call(functools.partial(kernel, n_store, n_feat), out_shape=outs...  117 us
    pallas_call x1, Pallas kernels, body(): pl.pallas_call(hand_over, out_shape=outs, in_specs=[pl.BlockSpec(memory_s...  30.9 us

profile of v5, /device:TPU:1, one launch (start us, length us, event | category | flops | bytes accessed | tf_op | source)
XLA Modules:
  0.0 148.5 jit_solution(14537225075326067392)
XLA Ops:
  0.6 117.0 %shard_map.137 = (bf16[64,512]{1,0:T(8,128)(2,1)}, f32[48,1024]{1,0:T(8,128)}, f32[48,1024]{1,0:T(8,128)}, f32[64,1024]{1,0:T(8,128)}, f32[64,1024]{1,0:T(8,128)}) custom-call(f32[48,4096]{1,0:T(8,128)} %features_hbm.1, s32[1,32,256]{2,1,0:T(8,128)} %serve_rows_hbm.1, s32[1,32]{1,0:T(1,128)} %row_counts_hbm.1, s32[11,1,512]{2,1,0:T(1,128)} %bitcast.1, ...), custom_call_target="tpu_custom_call" | custom-call | tf_op jit(solution)/shard_map/pallas_call | solution.py:759
  117.6 30.9 %shard_map.138 = (bf16[64,512]{1,0:T(8,128)(2,1)}, f32[48,1024]{1,0:T(8,128)}, f32[48,1024]{1,0:T(8,128)}, f32[64,1024]{1,0:T(8,128)}, f32[64,1024]{1,0:T(8,128)}) custom-call(bf16[64,512]{1,0:T(8,128)(2,1)} %get-tuple-element.10.refs_0_, f32[48,1024]{1,0:T(8,128)} %get-tuple-element.11.refs_1_, f32[48,1024]{1,0:T(8,128)} %get-tuple-element.12.refs_2_, ...), custom_call_target="tpu_custom_call" | custom-call | tf_op jit(solution)/shard_map/pallas_call | solution.py:767

commit v6 on v5

--- a/solution.py
+++ b/solution.py
@@ -174,6 +174,15 @@
 
         lax.fori_loop(low, high, step, 0)
 
+    def each_chip(fn):
+        fn(chip_peer(n_chip // 2))
+
+        def pair(i):
+            fn(chip_peer(n_chip // 2 - i))
+            fn(chip_peer(i - n_chip // 2))
+
+        loop(1, n_chip // 2, pair)
+
     def share(src_of, dst, name):
         loop(1, n_feat, lambda k: send(src_of(feat_peer(k)), dst, name, recv_of(name), "feat", feat_peer(k)))
         keep(src_of(my_feat), dst, recv_of(name))
@@ -288,7 +297,11 @@
             total = jnp.where(high_of == high, found[high * width : (high + 1) * width, :], total)
         stage[trainer] = total.astype(BF16)
 
-    loop(0, n_store, serve)
+    def serve_two(i):
+        serve(2 * i)
+        serve(2 * i + 1)
+
+    loop(0, n_store // 2, serve_two)
     for read in reads[2:]:
         read.wait()
     pl.semaphore_wait(barrier, n_store + n_feat - 2)
@@ -458,9 +471,7 @@
                 both_cores = part[pl.ds(my_core * tiles, tiles)].astype(F32) + merged[0:tiles].astype(F32)
                 merged[tiles : 2 * tiles] = both_cores.astype(BF16)
 
-            def to(k):
-                chip = chip_peer(k)
-
+            def to(chip):
                 @pl.when(sums(chip))
                 def _():
                     send(
@@ -472,7 +483,7 @@
                         chip * 2 + my_core,
                     )
 
-            loop(1, n_chip, to)
+            each_chip(to)
 
             def sent():
                 for count, wait_here in ((summers - 1, sums(my_chip)), (summers, jnp.logical_not(sums(my_chip)))):
@@ -500,17 +511,15 @@
                     summed += arrived[chip * per : (chip + 1) * per].astype(F32)
                 at = pl.ds(my_core * tiles + first(my_chip), per)
                 total[at] = summed.astype(BF16)
-                loop(
-                    1,
-                    n_chip,
-                    lambda k: send(
+                each_chip(
+                    lambda chip: send(
                         total.at[at],
                         total.at[at],
                         name + "_spread",
                         recv_of(name + "_spread"),
                         "store",
-                        chip_peer(k) * 2 + my_core,
-                    ),
+                        chip * 2 + my_core,
+                    )
                 )
 
             def sent():
@@ -672,10 +681,15 @@
 
 
 def hand_over(*refs):
-    copies = [pltpu.make_async_copy(refs[i], refs[5 + i], refs[10].at[i]) for i in range(5)]
-    for copy in copies:
+    src, dst, held, sems = refs[:5], refs[5:10], refs[10:15], refs[15]
+    reads = [pltpu.make_async_copy(src[i], held[i], sems.at[i]) for i in range(5)]
+    writes = [pltpu.make_async_copy(held[i], dst[i], sems.at[5 + i]) for i in range(5)]
+    for read in reads:
+        read.start()
+    for read, copy in zip(reads, writes):
+        read.wait()
         copy.start()
-    for copy in copies:
+    for copy in writes:
         copy.wait()
 
 
@@ -769,7 +783,7 @@
         out_shape=outs,
         in_specs=[pl.BlockSpec(memory_space=pltpu.HBM)] * 5,
         out_specs=[pl.BlockSpec(memory_space=pltpu.HBM)] * 5,
-        scratch_shapes=[pltpu.SemaphoreType.DMA((5,))],
+        scratch_shapes=[pltpu.VMEM(out.shape, out.dtype) for out in outs] + [pltpu.SemaphoreType.DMA((10,))],
         compiler_params=pltpu.CompilerParams(vmem_limit_bytes=VMEM_LIMIT),
     )(*found)
 

time: 149 us -> 116 us (0.78)
  Pallas kernels: 148 us -> 115 us
    pallas_call x1, Pallas kernels: 30.9 us -> 2.06 us  [body(): pl.pallas_call(hand_over, out_shape=outs, in_specs=[pl.BlockSpec(memory_s...]
    pallas_call x1, Pallas kernels: 117 us -> 113 us  [body(): pl.pallas_call(functools.partial(kernel, n_store, n_feat), out_shape=outs...]
where the time goes in v6:
time: 116 us
  Pallas kernels  115 us (99%)
    pallas_call x1, Pallas kernels, body(): pl.pallas_call(functools.partial(kernel, n_store, n_feat), out_shape=outs...  113 us

profile of v6, /device:TPU:1, one launch (start us, length us, event | category | flops | bytes accessed | tf_op | source)
XLA Modules:
  0.0 115.9 jit_solution(8963162562514388827)
XLA Ops:
  0.6 113.2 %shard_map.137 = (bf16[64,512]{1,0:T(8,128)(2,1)}, f32[48,1024]{1,0:T(8,128)}, f32[48,1024]{1,0:T(8,128)}, f32[64,1024]{1,0:T(8,128)}, f32[64,1024]{1,0:T(8,128)}) custom-call(f32[48,4096]{1,0:T(8,128)} %features_hbm.1, s32[1,32,256]{2,1,0:T(8,128)} %serve_rows_hbm.1, s32[1,32]{1,0:T(1,128)} %row_counts_hbm.1, s32[11,1,512]{2,1,0:T(1,128)} %bitcast.1, ...), custom_call_target="tpu_custom_call" | custom-call | tf_op jit(solution)/shard_map/pallas_call | solution.py:773
  113.8 2.1 %shard_map.138 = (bf16[64,512]{1,0:T(8,128)(2,1)}, f32[48,1024]{1,0:T(8,128)}, f32[48,1024]{1,0:T(8,128)}, f32[64,1024]{1,0:T(8,128)}, f32[64,1024]{1,0:T(8,128)}) custom-call(bf16[64,512]{1,0:T(8,128)(2,1)} %get-tuple-element.10.refs_0_, f32[48,1024]{1,0:T(8,128)} %get-tuple-element.11.refs_1_, f32[48,1024]{1,0:T(8,128)} %get-tuple-element.12.refs_2_, ...), custom_call_target="tpu_custom_call" | custom-call | tf_op jit(solution)/shard_map/pallas_call | solution.py:781

commit v7 on v6

--- a/solution.py
+++ b/solution.py
@@ -174,6 +174,9 @@
 
         lax.fori_loop(low, high, step, 0)
 
+    def far_first(n):
+        return sorted(range(1, n), key=lambda k: -min(k, n - k))
+
     def each_chip(fn):
         fn(chip_peer(n_chip // 2))
 
@@ -184,7 +187,11 @@
         loop(1, n_chip // 2, pair)
 
     def share(src_of, dst, name):
-        loop(1, n_feat, lambda k: send(src_of(feat_peer(k)), dst, name, recv_of(name), "feat", feat_peer(k)))
+        for down in far_first(n_y) + [0]:
+            for right in far_first(n_x) + [0]:
+                if down or right:
+                    peer = lax.rem(my_y + down, n_y) * n_x + lax.rem(my_x + right, n_x)
+                    send(src_of(peer), dst, name, recv_of(name), "feat", peer)
         keep(src_of(my_feat), dst, recv_of(name))
 
     def along(x, k):
@@ -195,7 +202,8 @@
 
     def spread_near(name, own, dst, x):
         step, spot = name + "_near", dst.at[my_y, my_x]
-        loop(1, count_of(x), lambda k: send(own, spot, step, recv_of(step), "feat", along(x, k)))
+        for k in far_first(count_of(x)):
+            send(own, spot, step, recv_of(step), "feat", along(x, k))
         keep(own, spot, recv_of(step))
         if count_of(x) > 1:
             later(dst.at[0, pl.ds(0, n_x - 1)] if x else dst.at[pl.ds(0, n_y - 1), 0], step)
@@ -203,7 +211,8 @@
     def spread_far(name, dst, x):
         step, line = name + "_far", dst.at[my_y] if x else dst.at[:, my_x]
         await_bytes(line, recv_of(name + "_near"))
-        loop(1, count_of(not x), lambda k: send(line, line, step, recv_of(step), "feat", along(not x, k)))
+        for k in far_first(count_of(not x)):
+            send(line, line, step, recv_of(step), "feat", along(not x, k))
         if count_of(not x) > 1:
             later(dst.at[pl.ds(0, n_y - 1)] if x else dst.at[:, pl.ds(0, n_x - 1)], step)
 
@@ -217,7 +226,8 @@
         def lines(k):
             return src.at[:, lax.rem(my_x + k, n_x)] if x else src.at[lax.rem(my_y + k, n_y)]
 
-        loop(1, count_of(x), lambda k: send(lines(k), dst.at[mine], step, recv_of(step), "feat", along(x, k)))
+        for k in far_first(count_of(x)):
+            send(lines(k), dst.at[mine], step, recv_of(step), "feat", along(x, k))
         keep(lines(0), dst.at[mine], recv_of(step))
         if count_of(x) > 1:
             later(dst.at[pl.ds(0, count_of(x) - 1)], step)
@@ -233,7 +243,8 @@
         def block(k):
             return middle.at[lax.rem(my_y + k, n_y) if x else lax.rem(my_x + k, n_x)]
 
-        loop(1, count_of(not x), lambda k: send(block(k), dst.at[mine], step, recv_of(step), "feat", along(not x, k)))
+        for k in far_first(count_of(not x)):
+            send(block(k), dst.at[mine], step, recv_of(step), "feat", along(not x, k))
         keep(block(0), dst.at[mine], recv_of(step))
         if count_of(not x) > 1:
             later(dst.at[pl.ds(0, count_of(not x) - 1)], step)
@@ -297,11 +308,11 @@
             total = jnp.where(high_of == high, found[high * width : (high + 1) * width, :], total)
         stage[trainer] = total.astype(BF16)
 
-    def serve_two(i):
-        serve(2 * i)
-        serve(2 * i + 1)
-
-    loop(0, n_store // 2, serve_two)
+    def serve_some(i):
+        for j in range(4):
+            serve(4 * i + j)
+
+    loop(0, n_store // 4, serve_some)
     for read in reads[2:]:
         read.wait()
     pl.semaphore_wait(barrier, n_store + n_feat - 2)
@@ -575,7 +586,8 @@
                     device_id_type=MESH,
                 ).start()
 
-            loop(1, count_of(x), to_line)
+            for k in far_first(count_of(x)):
+                to_line(k)
             if count_of(x) > 1:
                 later(slope_all.at[0, 0, 0, pl.ds(0, n_x - 1)] if x else slope_all.at[0, 0, pl.ds(0, n_y - 1), 0], step)
 
@@ -607,7 +619,8 @@
             def forward(x=x):
                 line = slope_line(stage_no, x)
                 await_bytes(line, recv_of(f"slope{stage_no}_near"))
-                loop(1, count_of(not x), lambda k: send(line, line, step, recv_of(step), "feat", along(not x, k)))
+                for k in far_first(count_of(not x)):
+                    send(line, line, step, recv_of(step), "feat", along(not x, k))
 
             on_core(core, forward)
 
@@ -646,9 +659,9 @@
     reduce_a()
     first_weights(1, fill_b)
     reduce_b()
-    swap2()
     spread_a()
     spread_b()
+    swap2()
     finish2()
     across = hidden // 128
     for part, out in enumerate((w2_self_out, w2_neigh_out)):

time: 116 us -> 114 us (0.983)
  Pallas kernels: 115 us -> 113 us
    pallas_call x1, Pallas kernels: 113 us -> 111 us  [body(): pl.pallas_call(functools.partial(kernel, n_store, n_feat), out_shape=outs...]
where the time goes in v7:
time: 114 us
  Pallas kernels  113 us (99%)
    pallas_call x1, Pallas kernels, body(): pl.pallas_call(functools.partial(kernel, n_store, n_feat), out_shape=outs...  111 us

profile of v7, /device:TPU:1, one launch (start us, length us, event | category | flops | bytes accessed | tf_op | source)
XLA Modules:
  0.0 114.1 jit_solution(8182164521401339319)
XLA Ops:
  0.6 111.4 %shard_map.137 = (bf16[64,512]{1,0:T(8,128)(2,1)}, f32[48,1024]{1,0:T(8,128)}, f32[48,1024]{1,0:T(8,128)}, f32[64,1024]{1,0:T(8,128)}, f32[64,1024]{1,0:T(8,128)}) custom-call(f32[48,4096]{1,0:T(8,128)} %features_hbm.1, s32[1,32,256]{2,1,0:T(8,128)} %serve_rows_hbm.1, s32[1,32]{1,0:T(1,128)} %row_counts_hbm.1, s32[11,1,512]{2,1,0:T(1,128)} %bitcast.1, ...), custom_call_target="tpu_custom_call" | custom-call | tf_op jit(solution)/shard_map/pallas_call | solution.py:786
  112.1 2.1 %shard_map.138 = (bf16[64,512]{1,0:T(8,128)(2,1)}, f32[48,1024]{1,0:T(8,128)}, f32[48,1024]{1,0:T(8,128)}, f32[64,1024]{1,0:T(8,128)}, f32[64,1024]{1,0:T(8,128)}) custom-call(bf16[64,512]{1,0:T(8,128)(2,1)} %get-tuple-element.10.refs_0_, f32[48,1024]{1,0:T(8,128)} %get-tuple-element.11.refs_1_, f32[48,1024]{1,0:T(8,128)} %get-tuple-element.12.refs_2_, ...), custom_call_target="tpu_custom_call" | custom-call | tf_op jit(solution)/shard_map/pallas_call | solution.py:794
